TPU v7x, 128 devices: a whole 4x4x4 slice. The times are simulated.
128 devices in a mesh: freq: 32 (over z, x_lo, y), pair: 4 (over x_hi, core).
Axes of the slice: x: 4 (x_hi: 2, x_lo: 2; x = x_hi * 2 + x_lo), y: 4, z: 4, core: 2. Of those that a mesh axis runs over, the one named last changes fastest.
Arguments:
- voltages: bfloat16 [2048, 50304], P(('freq', 'pair')), may hold values from -90 to 90
- input_alive_mask: int32 [2048], P(('freq', 'pair')), may hold values 0 or 1
- pair_table: int32 [36, 2], P('pair'), may hold values from 0 to 7, as said below
Outputs:
- visibilities: bfloat16 [36, 96, 2, 256, 256], P('pair', 'freq')
Inputs may be any that keep to these rules, and one draw needn't show every extreme that they name: `pair_table`: each row holds a row block a and a column block b of the 8 blocks with a <= b; every such pair stands in exactly one row.
All inputs are finite; a program needn't handle non-finite values. No bound on the sum of `input_alive_mask` on one device may be relied on, other than what follows from the above.
Results may differ from a plain program's by a relative error of at most 0.0055.
Values may be sent and summed in bfloat16 or wider, within the bound.
A program may use at most 64 MiB of HBM per device.

v0:
```python
import math

import jax
import jax.numpy as jnp
from jax import lax
from jax.sharding import PartitionSpec as P

CHAN = 192
BAND = 96
TAPS = 4
SPECTRA = 128
BLOCK_INPUTS = 256


def filter_window(tap_count, period):
    length = tap_count * period
    sample_index = jnp.arange(length, dtype=jnp.float32)
    shape_part = jnp.sinc((sample_index - length / 2 + 0.5) / period)
    tapering = 0.54 - 0.46 * jnp.cos(2.0 * math.pi * sample_index / (length - 1))
    return (shape_part * tapering).reshape(tap_count, period)


def dft_table(channels, period):
    freq_index = lax.broadcasted_iota(jnp.int32, (channels, period), 0)
    time_index = lax.broadcasted_iota(jnp.int32, (channels, period), 1)
    phases = 2.0 * math.pi / period * (freq_index * time_index % period).astype(jnp.float32)
    return jnp.concatenate([jnp.cos(phases), -jnp.sin(phases)], axis=0)


def body(voltages, input_alive_mask, pair_table):
    inputs_dev = voltages.shape[0]
    period = 2 * CHAN
    frames = voltages.shape[1] // period
    samples = voltages.astype(jnp.float32).reshape(inputs_dev, frames, period)
    window = filter_window(TAPS, period)
    filtered = window[0] * samples[:, 0:SPECTRA, :]
    for tap_index in range(1, TAPS):
        filtered = filtered + window[tap_index] * samples[:, tap_index : tap_index + SPECTRA, :]
    spectrum = jnp.einsum(
        "kp,isp->kis", dft_table(BAND, period), filtered, precision=lax.Precision.HIGH
    )
    spectrum = spectrum.reshape(2, BAND, inputs_dev, SPECTRA)
    band_power = jnp.mean(spectrum[0] * spectrum[0] + spectrum[1] * spectrum[1], axis=2)
    gains = lax.rsqrt(band_power + 1e-06) * input_alive_mask.astype(jnp.float32)[None, :]
    equalized = (spectrum * gains[None, :, :, None]).astype(jnp.bfloat16)
    groups = lax.axis_size("freq")
    quarters = lax.axis_size("pair")
    channels_dev = BAND // groups
    spread = jnp.broadcast_to(
        equalized.reshape(2, groups, 1, channels_dev, inputs_dev, SPECTRA),
        (2, groups, quarters, channels_dev, inputs_dev, SPECTRA),
    ).reshape(2, groups * quarters * channels_dev, inputs_dev, SPECTRA)
    gathered = lax.all_to_all(spread, ("freq", "pair"), split_axis=1, concat_axis=2, tiled=True)
    inverse = 1.0 / SPECTRA

    def correlate(unused, pair_row):
        row_data = lax.dynamic_slice_in_dim(gathered, pair_row[0] * BLOCK_INPUTS, BLOCK_INPUTS, 2)
        col_data = lax.dynamic_slice_in_dim(gathered, pair_row[1] * BLOCK_INPUTS, BLOCK_INPUTS, 2)
        real_part = jnp.einsum(
            "cks,cls->ckl", row_data[0], col_data[0], preferred_element_type=jnp.float32
        )
        real_part = real_part + jnp.einsum(
            "cks,cls->ckl", row_data[1], col_data[1], preferred_element_type=jnp.float32
        )
        imag_part = jnp.einsum(
            "cks,cls->ckl", row_data[1], col_data[0], preferred_element_type=jnp.float32
        )
        imag_part = imag_part - jnp.einsum(
            "cks,cls->ckl", row_data[0], col_data[1], preferred_element_type=jnp.float32
        )
        vis_block = (jnp.stack([real_part, imag_part], axis=1) * inverse).astype(jnp.bfloat16)
        return (unused, vis_block)

    _, vis_blocks = lax.scan(correlate, jnp.zeros((), jnp.int32), pair_table)
    return vis_blocks


def solution(mesh):
    in_specs = (P(("freq", "pair"), None), P(("freq", "pair")), P("pair", None))
    out_specs = P("pair", "freq", None, None, None)
    return jax.shard_map(body, mesh=mesh, in_specs=in_specs, out_specs=out_specs, check_vma=False)
```

profile of v0, /device:TPU:1, one launch (start us, length us, event | category | flops | bytes accessed | tf_op | source)
XLA Modules:
  0.0 139.4 jit_solution(7780782980508891883)
XLA Ops:
  0.1 1.3 sine_negate_fusion
  1.4 1.8 %reshape.113 = f32[16,131,384]{2,1,0:T(8,128)S(1)} reshape(bf16[16,50304]{1,0:T(8,128)(2,1)} %param.5) | data formatting | bytes 4829184 | tf_op jit(solution)/shard_map/reshape | solution.py:34
  3.2 3.8 %fusion.10 = f32[192,16,128]{2,0,1:T(8,128)S(1)} fusion(f32[16,131,384]{2,1,0:T(8,128)S(1)} %reshape.113, f32[384]{0:T(512)S(1)} %get-tuple-element.39, f32[384]{0:T(512)S(1)} %get-tuple-element.40, f32[384]{0:T(512)S(1)} %get-tuple-element.41, f32[384]{0:T(512)S(1)} %get-tuple-element.38, f32[96,384]{1,0:T(8,128)S(1)} %get-tuple-element.42, ...), kind=kOutput, calls=%fused_computation.20 | convolution fusion | flops 911548416 | bytes 14458880 | tf_op jit(solution)/shard_map/kp,isp->kis/dot_general | solution.py:39
  7.0 0.9 copy.11
  7.9 0.3 fusion.21
  8.9 2.2 %broadcast_in_dim.18 = bf16[2,32,4,3,16,128]{5,4,0,3,2,1:T(8,128)(2,1)} broadcast(bf16[2,32,3,16,128]{4,3,0,2,1:T(8,128)(2,1)S(1)} %copy.13), dimensions={0,1,3,4,5} | broadcast | bytes 3932160 | tf_op jit(solution)/shard_map/broadcast_in_dim | solution.py:49
  11.1 11.5 %all-to-all-start = ((bf16[2,384,16,128]{3,2,0,1:T(8,128)(2,1)}), bf16[2,384,16,128]{3,2,0,1:T(8,128)(2,1)S(1)}, u32[]{:S(2)}, u32[]{:S(2)}) async-start(bf16[2,384,16,128]{3,2,0,1:T(8,128)(2,1)} %bitcast.57), calls=%async_computation | async-start | bytes 6291456 | tf_op jit(solution)/shard_map/all_to_all | solution.py:53
  22.6 41.3 %all-to-all-done = bf16[2,384,16,128]{3,2,0,1:T(8,128)(2,1)S(1)} async-done(((bf16[2,384,16,128]{3,2,0,1:T(8,128)(2,1)}), bf16[2,384,16,128]{3,2,0,1:T(8,128)(2,1)S(1)}, u32[]{:S(2)}, u32[]{:S(2)}) %all-to-all-start) | async-done | bytes 3145760 | tf_op jit(solution)/shard_map/all_to_all | solution.py:53
  63.9 2.2 %copy.15 = bf16[2,3,128,16,128]{4,3,2,1,0:T(8,128)(2,1)} copy(bf16[2,3,128,16,128]{4,3,0,1,2:T(8,128)(2,1)S(1)} %bitcast.56) | data formatting | bytes 6291456 | tf_op jit(solution)/shard_map/all_to_all | solution.py:53
  66.1 73.3 %while.10 = (s32[]{:T(128)}, bf16[9,3,2,256,256]{4,3,2,1,0:T(8,128)(2,1)}, s32[9,2]{0,1:T(2,128)S(1)}, bf16[2,3,2048,128]{3,2,1,0:T(8,128)(2,1)}, s32[]{:T(128)}...) while((s32[]{:T(128)}, bf16[9,3,2,256,256]{4,3,2,1,0:T(8,128)(2,1)}, s32[9,2]{0,1:T(2,128)S(1)}, ...), condition=%wide.region_2.3_spmd, body=%wide.region_1.2_spmd.sunk | while | flops 202899456 | bytes 8653577 | solution.py:74
  66.2 0.6 fusion.69
  68.0 1.3 fusion.72
  69.3 1.3 fusion.73
  70.6 1.3 fusion.70
  71.9 1.3 fusion.71
  73.2 1.0 copy_dynamic-update-slice_fusion.2
  74.3 0.6 fusion.69
  76.2 1.3 fusion.72
  77.5 1.3 fusion.73
  78.8 1.3 fusion.70
  80.1 1.3 fusion.71
  81.4 1.0 copy_dynamic-update-slice_fusion.2
  82.5 0.6 fusion.69
  84.3 1.3 fusion.72
  85.6 1.3 fusion.73
  86.9 1.3 fusion.70
  88.2 1.3 fusion.71
  89.5 1.0 copy_dynamic-update-slice_fusion.2
  90.6 0.6 fusion.69
  92.4 1.3 fusion.72
  93.7 1.3 fusion.73
  95.0 1.3 fusion.70
  96.3 1.3 fusion.71
  97.6 1.0 copy_dynamic-update-slice_fusion.2
  98.7 0.6 fusion.69
  100.6 1.3 fusion.72
  101.9 1.3 fusion.73
  103.2 1.3 fusion.70
  104.5 1.3 fusion.71
  105.8 1.0 copy_dynamic-update-slice_fusion.2
  106.9 0.6 fusion.69
  108.7 1.3 fusion.72
  110.0 1.3 fusion.73
  111.3 1.3 fusion.70
  112.6 1.3 fusion.71
  113.9 1.0 copy_dynamic-update-slice_fusion.2
  115.0 0.6 fusion.69
  116.9 1.3 fusion.72
  118.2 1.3 fusion.73
  119.5 1.3 fusion.70
  120.8 1.3 fusion.71
  122.1 1.0 copy_dynamic-update-slice_fusion.2
  123.2 0.6 fusion.69
  125.0 1.3 fusion.72
  126.3 1.3 fusion.73
  127.6 1.3 fusion.70
  128.9 1.3 fusion.71
  130.2 1.0 copy_dynamic-update-slice_fusion.2
  131.3 0.6 fusion.69
  133.2 1.3 fusion.72
  134.5 1.3 fusion.73
  135.8 1.3 fusion.70
  137.1 1.3 fusion.71
  138.4 1.0 copy_dynamic-update-slice_fusion.2
  (23 shorter events, 1.3 us)
Async XLA Ops:
  7.0 1.4 %copy-start.1 = (s32[16]{0:T(128)S(1)}, s32[16]{0:T(128)}, u32[]{:S(2)}) copy-start(s32[16]{0:T(128)} %param.6) | copy-start | bytes 196
  11.1 52.8 %all-to-all-start = ((bf16[2,384,16,128]{3,2,0,1:T(8,128)(2,1)}), bf16[2,384,16,128]{3,2,0,1:T(8,128)(2,1)S(1)}, u32[]{:S(2)}, u32[]{:S(2)}) async-start(bf16[2,384,16,128]{3,2,0,1:T(8,128)(2,1)} %bitcast.57), calls=%async_computation | async-start | bytes 6291456 | tf_op jit(solution)/shard_map/all_to_all | solution.py:53
  63.9 2.2 %copy-start = (s32[9,2]{0,1:T(2,128)S(1)}, s32[9,2]{0,1:T(2,128)}, u32[]{:S(2)}) copy-start(s32[9,2]{0,1:T(2,128)} %param.7) | copy-start | bytes 220
where the time goes:
time: 140 us; the launch traced here: 139 us
  matrix products  50.4 us (36%)
  waiting for transfers between devices  41.3 us (30%)
  local copies, waits for them, and re-layouts  13.3 us (10%)
  starting transfers between devices  11.5 us (8%)
  loops' own time  11.5 us (8%)
  other arithmetic  11.2 us (8%)
    all_to_all x1, waiting for transfers between devices, body(): lax.all_to_all(spread, ('freq', 'pair'), split_axis=1, concat_axis=2, til...  41.3 us
    dot_general x9, matrix products, correlate(): jnp.einsum('cks,cls->ckl', row_data[1], col_data[1], preferred_element_ty...  11.7 us
    dot_general x9, matrix products, correlate(): jnp.einsum('cks,cls->ckl', row_data[0], col_data[1], preferred_element_ty...  11.6 us
    dot_general x9, matrix products, correlate(): jnp.einsum('cks,cls->ckl', row_data[1], col_data[0], preferred_element_ty...  11.6 us
    dot_general x9, matrix products, correlate(): jnp.einsum('cks,cls->ckl', row_data[0], col_data[0], preferred_element_ty...  11.6 us
    another operation x1, loops' own time, body(): _, vis_blocks = lax.scan(correlate, jnp.zeros((), jnp.int32), pair_table)  11.5 us
    all_to_all x1, starting transfers between devices, body(): lax.all_to_all(spread, ('freq', 'pair'), split_axis=1, concat_axis=2, til...  11.5 us
    dynamic_update_slice x9, other arithmetic, body(): _, vis_blocks = lax.scan(correlate, jnp.zeros((), jnp.int32), pair_table)  9.2 us
  transfers between devices with their start and end apart: 1, of which 1 were waited for; matrix products, arithmetic and copies ran while one was open for 0% of the time, Pallas kernels for 0%

commit v1 on v0

v1 whole, which is shorter than its diff:
```python
import functools
import math

import jax
import jax.numpy as jnp
import numpy as np
from jax import lax
from jax.experimental import pallas as pl
from jax.experimental.pallas import tpu as pltpu
from jax.sharding import PartitionSpec as P

CHAN = 192
BAND = 96
TAPS = 4
SPECTRA = 128
BLOCK = 256
PERIOD = 2 * CHAN
SIDE = 4
RINGS = SIDE * SIDE
LOCAL = 16
DEPTH = 3
GROUPS = BAND // DEPTH
MESH = pl.DeviceIdType.MESH

ORDER = (
    (1, 0), (0, 1), (3, 0), (0, 3), (2, 0), (0, 2), (1, 1), (3, 3),
    (1, 3), (3, 1), (2, 1), (1, 2), (2, 3), (3, 2), (2, 2),
)


def tables():
    length = TAPS * PERIOD
    j = np.arange(length, dtype=np.float64)
    window = np.sinc((j - length / 2 + 0.5) / PERIOD) * (0.54 - 0.46 * np.cos(2 * math.pi * j / (length - 1)))
    window = window.reshape(TAPS, PERIOD).astype(np.float32)
    z, y, q, ch = np.meshgrid(np.arange(4), np.arange(4), np.arange(2), np.arange(DEPTH), indexing="ij")
    k = ((z * 8 + q * 4 + y) * DEPTH + ch).reshape(-1)
    phase = 2 * math.pi / PERIOD * (k[:, None] * np.arange(PERIOD)[None, :] % PERIOD)
    rows = np.stack([np.cos(phase), -np.sin(phase)], axis=1).reshape(2 * BAND, PERIOD)
    high = rows.astype(jnp.bfloat16)
    low = (rows - high.astype(np.float64)).astype(jnp.bfloat16)
    return window, np.concatenate([high, low, high], axis=1)


def place():
    f, p = lax.axis_index("freq"), lax.axis_index("pair")
    z, x_lo, y = lax.div(f, 8), lax.rem(lax.div(f, 4), 2), lax.rem(f, 4)
    return z, lax.div(p, 2) * 2 + x_lo, y, lax.rem(p, 2)


def device(z, x, y, c):
    return (z * 8 + lax.rem(x, 2) * 4 + y, lax.div(x, 2) * 2 + c)


def slot(z, x, y, c):
    f, p = device(z, x, y, c)
    return f * 4 + p


def ahead(a, d):
    return lax.rem(a + d, SIDE)


def behind(a, d):
    return lax.rem(a + SIDE - d, SIDE)


def channelize(volts, window, dft, mask, fir, spec, ready):
    def filt(step, carry):
        first = step * 8
        frames = []
        for t in range(8 + TAPS - 1):
            at = pl.multiple_of((first + t) * PERIOD, 128)
            frames.append(volts[:, pl.ds(at, PERIOD)].astype(jnp.float32))
        for t in range(8):
            total = window[0:1, :] * frames[t]
            for m in range(1, TAPS):
                total = total + window[m : m + 1, :] * frames[t + m]
            row = pl.multiple_of((first + t) * LOCAL, LOCAL)
            for j in range(3):
                fir[j, pl.ds(row, LOCAL), :] = total[:, j * 128 : (j + 1) * 128]
        return carry

    lax.fori_loop(0, SPECTRA // 8, filt, 0)

    def transform(pair, carry):
        highs, lows = [], []
        for half in range(2):
            i = pair * 2 + half
            x = jnp.concatenate([fir[j, pl.ds(i, SPECTRA, stride=LOCAL), :] for j in range(3)], axis=1)
            high = x.astype(jnp.bfloat16)
            highs.append(high)
            lows.append((x - high.astype(jnp.float32)).astype(jnp.bfloat16))
        high, low = jnp.concatenate(highs, axis=0), jnp.concatenate(lows, axis=0)
        right = jnp.concatenate([high, high, low], axis=1)
        out = lax.dot_general(dft[...], right, (((1,), (1,)), ((), ())), preferred_element_type=jnp.float32)
        for half in range(2):
            i = pair * 2 + half
            spec[pl.ds(i, 2 * BAND, stride=LOCAL), :] = out[:, half * SPECTRA : (half + 1) * SPECTRA]
        return carry

    lax.fori_loop(0, LOCAL // 2, transform, 0)
    alive = mask[...].astype(jnp.float32)

    def equalize(ring, carry):
        for e in range(2 * DEPTH):
            at = pl.multiple_of((ring * 2 * DEPTH + e) * 2 * LOCAL, 2 * LOCAL)
            re, im = spec[pl.ds(at, LOCAL), :], spec[pl.ds(at + LOCAL, LOCAL), :]
            power = jnp.sum(re * re + im * im, axis=1, keepdims=True) * (1.0 / SPECTRA)
            gain = lax.rsqrt(power + 1e-06) * alive
            both = jnp.concatenate([re * gain, im * gain], axis=1)
            ready[ring, e // DEPTH, e % DEPTH] = both.astype(jnp.bfloat16)
        return carry

    lax.fori_loop(0, RINGS, equalize, 0)


def exchange_kernel(volts, window, dft, mask, out, fir, spec, ready, relay, s1, r1, s2, r2, s3, r3, sl):
    z, x, y, c = place()
    q = lax.rem(x, 2)
    barrier = pltpu.get_barrier_semaphore()
    peers = [device(ahead(z, dz), x, ahead(y, dy), c) for dz, dy in ORDER]
    peers += [device(z, ahead(x, d), y, c) for d in (1, 2, 3)] + [device(z, x, y, 1 - c)]
    for peer in peers:
        pl.semaphore_signal(barrier, inc=1, device_id=peer, device_id_type=MESH)

    channelize(volts, window, dft, mask, fir, spec, ready)

    pl.semaphore_wait(barrier, len(peers))
    sends = []

    def send(src, dst, send_sem, recv_sem, to):
        copy = pltpu.make_async_remote_copy(
            src_ref=src, dst_ref=dst, send_sem=send_sem, recv_sem=recv_sem, device_id=to, device_id_type=MESH
        )
        copy.start()
        sends.append(copy)

    def arrived(dst, sem):
        pltpu.make_async_copy(dst, dst, sem).wait()

    def spread(k, zs, ys, mine, others):
        at = slot(zs, x, ys, c)
        send(others, out.at[at], s2.at[3 * k + 1], r2.at[3 * k + 1], device(z, ahead(x, 1), y, c))
        send(others, out.at[at], s2.at[3 * k + 2], r2.at[3 * k + 2], device(z, ahead(x, 3), y, c))
        send(mine, out.at[at], s2.at[3 * k], r2.at[3 * k], device(z, ahead(x, 2), y, c))
        send(mine, out.at[at], s3.at[4 * k], r3.at[4 * k], device(z, x, y, 1 - c))

    here, own = z * SIDE + y, slot(z, x, y, c)
    spread(0, z, y, ready.at[here, q], ready.at[here, 1 - q])
    keep = pltpu.make_async_copy(ready.at[here, q], out.at[own], sl)
    keep.start()
    for k, (dz, dy) in enumerate(ORDER, 1):
        zd, yd = ahead(z, dz), ahead(y, dy)
        to, there = device(zd, x, yd, c), zd * SIDE + yd
        send(ready.at[there, 1 - q], relay.at[here], s1.at[2 * k + 1], r1.at[2 * k + 1], to)
        send(ready.at[there, q], out.at[own], s1.at[2 * k], r1.at[2 * k], to)
    for k, (dz, dy) in enumerate(ORDER, 1):
        zs, ys = behind(z, dz), behind(y, dy)
        at, ring = slot(zs, x, ys, c), zs * SIDE + ys
        arrived(relay.at[ring], r1.at[2 * k + 1])
        arrived(out.at[at], r1.at[2 * k])
        spread(k, zs, ys, out.at[at], relay.at[ring])
    for k, (dz, dy) in enumerate(((0, 0),) + ORDER):
        zs, ys = behind(z, dz), behind(y, dy)
        for j, d in ((1, 1), (2, 3), (0, 2)):
            at = slot(zs, behind(x, d), ys, c)
            arrived(out.at[at], r2.at[3 * k + j])
            send(out.at[at], out.at[at], s3.at[4 * k + 1 + j], r3.at[4 * k + 1 + j], device(z, x, y, 1 - c))
    for k, (dz, dy) in enumerate(((0, 0),) + ORDER):
        zs, ys = behind(z, dz), behind(y, dy)
        for j, d in ((-1, 0), (1, 1), (2, 3), (0, 2)):
            arrived(out.at[slot(zs, behind(x, d), ys, 1 - c)], r3.at[4 * k + 1 + j])
    for copy in sends:
        copy.wait_send()
    keep.wait()


def exchange(volts, window, dft, mask):
    dma = pltpu.SemaphoreType.DMA
    whole = pl.BlockSpec(memory_space=pltpu.VMEM)
    return pl.pallas_call(
        exchange_kernel,
        out_shape=jax.ShapeDtypeStruct((128, DEPTH, LOCAL, 2 * SPECTRA), jnp.bfloat16),
        in_specs=[whole] * 4,
        out_specs=pl.BlockSpec(memory_space=pl.ANY),
        scratch_shapes=[
            pltpu.VMEM((3, SPECTRA * LOCAL, 128), jnp.float32),
            pltpu.VMEM((2 * BAND * LOCAL, SPECTRA), jnp.float32),
            pltpu.VMEM((RINGS, 2, DEPTH, LOCAL, 2 * SPECTRA), jnp.bfloat16),
            pltpu.VMEM((RINGS, DEPTH, LOCAL, 2 * SPECTRA), jnp.bfloat16),
            dma((2 * RINGS,)),
            dma((2 * RINGS,)),
            dma((3 * RINGS,)),
            dma((3 * RINGS,)),
            dma((4 * RINGS,)),
            dma((4 * RINGS,)),
            dma,
        ],
        compiler_params=pltpu.CompilerParams(
            collective_id=0, has_side_effects=True, vmem_limit_bytes=32 * 1024 * 1024
        ),
        cost_estimate=pl.CostEstimate(flops=2 * 3 * 192 * 384 * 2048, bytes_accessed=6 << 20, transcendentals=1536),
        name="exchange",
    )(volts, window, dft, mask)


def correlate_kernel(rows, table, spectra, out):
    first = pl.program_id(1) * rows
    for r in range(rows):
        a, b = table[first + r, 0], table[first + r, 1]
        left = spectra[pl.ds(a * LOCAL, LOCAL), 0].reshape(BLOCK, 2 * SPECTRA)
        right = spectra[pl.ds(b * LOCAL, LOCAL), 0].reshape(BLOCK, 2 * SPECTRA)
        turned = jnp.concatenate([left[:, SPECTRA:], -left[:, :SPECTRA]], axis=1)
        for part, lhs in ((0, left), (1, turned)):
            vis = lax.dot_general(lhs, right, (((1,), (1,)), ((), ())), preferred_element_type=jnp.float32)
            out[r, 0, part] = (vis * (1.0 / SPECTRA)).astype(jnp.bfloat16)


def correlate(table, spectra):
    pairs, rows = table.shape[0], 3
    return pl.pallas_call(
        functools.partial(correlate_kernel, rows),
        out_shape=jax.ShapeDtypeStruct((pairs, DEPTH, 2, BLOCK, BLOCK), jnp.bfloat16),
        grid_spec=pltpu.PrefetchScalarGridSpec(
            num_scalar_prefetch=1,
            grid=(DEPTH, pairs // rows),
            in_specs=[pl.BlockSpec((128, 1, LOCAL, 2 * SPECTRA), lambda ch, p, table: (0, ch, 0, 0))],
            out_specs=pl.BlockSpec((rows, 1, 2, BLOCK, BLOCK), lambda ch, p, table: (p, ch, 0, 0, 0)),
        ),
        compiler_params=pltpu.CompilerParams(vmem_limit_bytes=32 * 1024 * 1024),
        cost_estimate=pl.CostEstimate(flops=2 * 54 * 256**3, bytes_accessed=10 << 20, transcendentals=0),
        name="correlate",
    )(table, spectra)


def body(voltages, input_alive_mask, pair_table):
    window, dft = tables()
    spectra = exchange(voltages, jnp.asarray(window), jnp.asarray(dft), input_alive_mask.reshape(LOCAL, 1))
    return correlate(pair_table, spectra)


def solution(mesh):
    in_specs = (P(("freq", "pair"), None), P(("freq", "pair")), P("pair", None))
    out_specs = P("pair", "freq", None, None, None)
    return jax.shard_map(body, mesh=mesh, in_specs=in_specs, out_specs=out_specs, check_vma=False)
```

time: 140 us -> 51.2 us (0.37)
  matrix products: 50.4 us -> 0 us
  Pallas kernels: 0 us -> 46.3 us
  waiting for transfers between devices: 41.3 us -> 0 us
  loops' own time: 11.5 us -> 0 us
  starting transfers between devices: 11.5 us -> 0 us
  other arithmetic: 11.2 us -> 0 us
  local copies, waits for them, and re-layouts: 13.3 us -> 4.62 us
    dot_general x37 -> x0, matrix products: 50.4 us -> none  [the longest x9 11.7 us: correlate(): jnp.einsum('cks,cls->ckl', row_data[1], col_data[1], preferred_element_ty...]
    pallas_call x0 -> x2, Pallas kernels: none -> 46.3 us  [the longest x1 39 us: exchange(): pl.pallas_call(exchange_kernel, out_shape=jax.ShapeDtypeStruct((128, DEPT...]
    all_to_all x1 -> x0, waiting for transfers between devices: 41.3 us -> none  [body(): lax.all_to_all(spread, ('freq', 'pair'), split_axis=1, concat_axis=2, til...]
    another operation x1 -> x0, loops' own time: 11.5 us -> none  [body(): _, vis_blocks = lax.scan(correlate, jnp.zeros((), jnp.int32), pair_table)]
    all_to_all x1 -> x0, starting transfers between devices: 11.5 us -> none  [body(): lax.all_to_all(spread, ('freq', 'pair'), split_axis=1, concat_axis=2, til...]
    dynamic_update_slice x9 -> x0, other arithmetic: 9.2 us -> none  [body(): _, vis_blocks = lax.scan(correlate, jnp.zeros((), jnp.int32), pair_table)]
    slice x10 -> x0, local copies, waits for them, and re-layouts: 5.32 us -> none  [the longest x9 5.32 us: correlate(): pair_row[0] * BLOCK_INPUTS]
    unnamed x4 -> x7, local copies, waits for them, and re-layouts: 0.01 us -> 3.89 us
  transfers between devices with their start and end apart: 1 -> 0, of which waited for: 1 -> 0; matrix products, arithmetic and copies ran while one was open for 0% -> 0% of each run, Pallas kernels for 0% -> 0%
where the time goes in v1:
time: 51.2 us; the launch traced here: 50.9 us
  Pallas kernels  46.3 us (90%)
  local copies, waits for them, and re-layouts  4.62 us (9%)
    pallas_call x1, Pallas kernels, exchange(): pl.pallas_call(exchange_kernel, out_shape=jax.ShapeDtypeStruct((128, DEPT...  39 us
    pallas_call x1, Pallas kernels, correlate(): pl.pallas_call(functools.partial(correlate_kernel, rows), out_shape=jax.S...  7.26 us
    unnamed x7, local copies, waits for them, and re-layouts  3.89 us

profile of v1, /device:TPU:1, one launch (start us, length us, event | category | flops | bytes accessed | tf_op | source)
XLA Modules:
  0.0 50.9 jit_solution(17060925082173542990)
XLA Ops:
  0.0 0.7 %copy.6.mask = s32[16,1]{1,0:T(8,128)S(1)} copy(s32[16,1]{0,1:T(1,128)} %bitcast.1) | data formatting | bytes 128 | tf_op jit(solution)/shard_map/reshape | solution.py:239
  0.7 0.8 %copy.7.table = s32[9,2]{1,0:T(8,128)S(1)} copy(s32[9,2]{0,1:T(2,128)} %param.7) | data formatting | bytes 144 | tf_op args[2]
  1.5 0.0 copy-start
  1.5 1.4 %copy-done = bf16[16,50304]{1,0:T(8,128)(2,1)S(1)} copy-done((bf16[16,50304]{1,0:T(8,128)(2,1)S(1)}, bf16[16,50304]{1,0:T(8,128)(2,1)}, u32[]{:S(2)}) %copy-start) | copy-done | bytes 1609752
  2.9 0.0 copy-start.1
  2.9 1.0 %copy-done.1 = bf16[192,1152]{1,0:T(8,128)(2,1)S(1)} copy-done((bf16[192,1152]{1,0:T(8,128)(2,1)S(1)}, bf16[192,1152]{1,0:T(8,128)(2,1)}, u32[]{:S(2)}) %copy-start.1) | copy-done | bytes 442392
  3.9 0.0 copy-start.2
  3.9 0.7 %copy-done.2 = f32[4,384]{1,0:T(4,128)S(1)} copy-done((f32[4,384]{1,0:T(4,128)S(1)}, f32[4,384]{1,0:T(4,128)}, u32[]{:S(2)}) %copy-start.2) | copy-done | bytes 6168
  4.6 39.0 %exchange.1.spectra = bf16[128,3,16,256]{3,2,1,0:T(8,128)(2,1)S(1)} custom-call(bf16[16,50304]{1,0:T(8,128)(2,1)S(1)} %copy-done, f32[4,384]{1,0:T(4,128)S(1)} %copy-done.2, bf16[192,1152]{1,0:T(8,128)(2,1)S(1)} %copy-done.1, s32[16,1]{1,0:T(8,128)S(1)} %copy.6.mask), custom_call_target="tpu_custom_call" | custom-call | flops 905969664 | bytes 6291456 | tf_op jit(solution)/shard_map/exchange/pallas_call | solution.py:182
  43.7 7.3 %correlate.1 = bf16[9,3,2,256,256]{4,3,2,1,0:T(8,128)(2,1)} custom-call(s32[9,2]{1,0:T(8,128)S(1)} %copy.7.table, bf16[128,3,16,256]{3,2,1,0:T(8,128)(2,1)S(1)} %exchange.1.spectra), custom_call_target="tpu_custom_call" | custom-call | flops 1811939328 | bytes 10485760 | tf_op jit(solution)/shard_map/correlate/pallas_call | solution.py:222
Async XLA Ops:
  1.5 1.4 %copy-start = (bf16[16,50304]{1,0:T(8,128)(2,1)S(1)}, bf16[16,50304]{1,0:T(8,128)(2,1)}, u32[]{:S(2)}) copy-start(bf16[16,50304]{1,0:T(8,128)(2,1)} %volts.1) | copy-start | bytes 4829188
  2.9 1.0 %copy-start.1 = (bf16[192,1152]{1,0:T(8,128)(2,1)S(1)}, bf16[192,1152]{1,0:T(8,128)(2,1)}, u32[]{:S(2)}) copy-start(bf16[192,1152]{1,0:T(8,128)(2,1)} %constant.5.clone.dft) | copy-start | bytes 1327108
  3.9 0.7 %copy-start.2 = (f32[4,384]{1,0:T(4,128)S(1)}, f32[4,384]{1,0:T(4,128)}, u32[]{:S(2)}) copy-start(f32[4,384]{1,0:T(4,128)} %constant.4.clone.window) | copy-start | bytes 18436

commit v2 on v1

--- a/solution.py
+++ b/solution.py
@@ -1,4 +1,3 @@
-import functools
 import math
 
 import jax
@@ -37,9 +36,9 @@
     k = ((z * 8 + q * 4 + y) * DEPTH + ch).reshape(-1)
     phase = 2 * math.pi / PERIOD * (k[:, None] * np.arange(PERIOD)[None, :] % PERIOD)
     rows = np.stack([np.cos(phase), -np.sin(phase)], axis=1).reshape(2 * BAND, PERIOD)
-    high = rows.astype(jnp.bfloat16)
-    low = (rows - high.astype(np.float64)).astype(jnp.bfloat16)
-    return window, np.concatenate([high, low, high], axis=1)
+    high = rows.astype(jnp.bfloat16).astype(np.float64)
+    low = (rows - high).astype(jnp.bfloat16)
+    return np.concatenate([high, low.astype(np.float64), window, np.zeros((8 - TAPS, PERIOD))]).astype(np.float32)
 
 
 def place():
@@ -65,29 +64,54 @@
     return lax.rem(a + SIDE - d, SIDE)
 
 
-def channelize(volts, window, dft, mask, fir, spec, ready):
+CHUNKS = 4
+STEP = SPECTRA // CHUNKS
+PITCH = LOCAL + 8
+
+
+def chunk(c):
+    first = 0 if c == 0 else c * STEP + TAPS - 1
+    return pl.ds(first * PERIOD, ((c + 1) * STEP + TAPS - 1 - first) * PERIOD)
+
+
+def channelize(volts_hbm, table_hbm, mask, volts, table, dft, fir, spec, ready, load):
+    loads = [pltpu.make_async_copy(table_hbm, table, load.at[CHUNKS])]
+    for c in range(CHUNKS):
+        loads.append(pltpu.make_async_copy(volts_hbm.at[:, chunk(c)], volts.at[:, chunk(c)], load.at[c]))
+    loads[1].start()
+    loads[0].start()
+    for part in loads[2:]:
+        part.start()
+    loads[0].wait()
+    rows = 2 * BAND
+    dft[:, 0:PERIOD] = table[0:rows].astype(jnp.bfloat16)
+    dft[:, PERIOD : 2 * PERIOD] = table[rows : 2 * rows].astype(jnp.bfloat16)
+    dft[:, 2 * PERIOD :] = dft[:, 0:PERIOD]
+
     def filt(step, carry):
         first = step * 8
         frames = []
         for t in range(8 + TAPS - 1):
             at = pl.multiple_of((first + t) * PERIOD, 128)
             frames.append(volts[:, pl.ds(at, PERIOD)].astype(jnp.float32))
+        window = [table[2 * rows + m : 2 * rows + m + 1, :] for m in range(TAPS)]
         for t in range(8):
-            total = window[0:1, :] * frames[t]
+            total = window[0] * frames[t]
             for m in range(1, TAPS):
-                total = total + window[m : m + 1, :] * frames[t + m]
-            row = pl.multiple_of((first + t) * LOCAL, LOCAL)
+                total = total + window[m] * frames[t + m]
+            row = pl.multiple_of((first + t) * PITCH, 8)
             for j in range(3):
                 fir[j, pl.ds(row, LOCAL), :] = total[:, j * 128 : (j + 1) * 128]
         return carry
 
-    lax.fori_loop(0, SPECTRA // 8, filt, 0)
-
-    def transform(pair, carry):
+    for c in range(CHUNKS):
+        loads[1 + c].wait()
+        lax.fori_loop(c * STEP // 8, (c + 1) * STEP // 8, filt, 0, unroll=True)
+
+    for pair in range(LOCAL // 2):
         highs, lows = [], []
-        for half in range(2):
-            i = pair * 2 + half
-            x = jnp.concatenate([fir[j, pl.ds(i, SPECTRA, stride=LOCAL), :] for j in range(3)], axis=1)
+        for i in (2 * pair, 2 * pair + 1):
+            x = jnp.concatenate([fir[j, pl.ds(i, SPECTRA, stride=PITCH), :] for j in range(3)], axis=1)
             high = x.astype(jnp.bfloat16)
             highs.append(high)
             lows.append((x - high.astype(jnp.float32)).astype(jnp.bfloat16))
@@ -95,12 +119,12 @@
         right = jnp.concatenate([high, high, low], axis=1)
         out = lax.dot_general(dft[...], right, (((1,), (1,)), ((), ())), preferred_element_type=jnp.float32)
         for half in range(2):
-            i = pair * 2 + half
-            spec[pl.ds(i, 2 * BAND, stride=LOCAL), :] = out[:, half * SPECTRA : (half + 1) * SPECTRA]
-        return carry
-
-    lax.fori_loop(0, LOCAL // 2, transform, 0)
-    alive = mask[...].astype(jnp.float32)
+            spec[pl.ds(2 * pair + half, rows, stride=LOCAL), :] = out[:, half * SPECTRA : (half + 1) * SPECTRA]
+
+    inputs = lax.broadcasted_iota(jnp.int32, (LOCAL, 1), 0)
+    alive = jnp.zeros((LOCAL, 1), jnp.float32)
+    for i in range(LOCAL):
+        alive = jnp.where(inputs == i, mask[i].astype(jnp.float32), alive)
 
     def equalize(ring, carry):
         for e in range(2 * DEPTH):
@@ -112,10 +136,12 @@
             ready[ring, e // DEPTH, e % DEPTH] = both.astype(jnp.bfloat16)
         return carry
 
-    lax.fori_loop(0, RINGS, equalize, 0)
-
-
-def exchange_kernel(volts, window, dft, mask, out, fir, spec, ready, relay, s1, r1, s2, r2, s3, r3, sl):
+    lax.fori_loop(0, RINGS, equalize, 0, unroll=4)
+
+
+def exchange_kernel(
+    volts_hbm, table_hbm, mask, out, volts, table, dft, fir, spec, ready, relay, load, s1, r1, s2, r2, s3, r3, sl
+):
     z, x, y, c = place()
     q = lax.rem(x, 2)
     barrier = pltpu.get_barrier_semaphore()
@@ -124,7 +150,7 @@
     for peer in peers:
         pl.semaphore_signal(barrier, inc=1, device_id=peer, device_id_type=MESH)
 
-    channelize(volts, window, dft, mask, fir, spec, ready)
+    channelize(volts_hbm, table_hbm, mask, volts, table, dft, fir, spec, ready, load)
 
     pl.semaphore_wait(barrier, len(peers))
     sends = []
@@ -176,19 +202,23 @@
     keep.wait()
 
 
-def exchange(volts, window, dft, mask):
+def exchange(volts, table, mask):
     dma = pltpu.SemaphoreType.DMA
-    whole = pl.BlockSpec(memory_space=pltpu.VMEM)
+    anywhere = pl.BlockSpec(memory_space=pltpu.HBM)
     return pl.pallas_call(
         exchange_kernel,
-        out_shape=jax.ShapeDtypeStruct((128, DEPTH, LOCAL, 2 * SPECTRA), jnp.bfloat16),
-        in_specs=[whole] * 4,
+        out_shape=pltpu.VMEM((128, DEPTH, LOCAL, 2 * SPECTRA), jnp.bfloat16),
+        in_specs=[anywhere, anywhere, pl.BlockSpec(memory_space=pltpu.SMEM)],
         out_specs=pl.BlockSpec(memory_space=pl.ANY),
         scratch_shapes=[
-            pltpu.VMEM((3, SPECTRA * LOCAL, 128), jnp.float32),
+            pltpu.VMEM(volts.shape, jnp.bfloat16),
+            pltpu.VMEM(table.shape, jnp.float32),
+            pltpu.VMEM((2 * BAND, 3 * PERIOD), jnp.bfloat16),
+            pltpu.VMEM((3, SPECTRA * PITCH, 128), jnp.float32),
             pltpu.VMEM((2 * BAND * LOCAL, SPECTRA), jnp.float32),
             pltpu.VMEM((RINGS, 2, DEPTH, LOCAL, 2 * SPECTRA), jnp.bfloat16),
             pltpu.VMEM((RINGS, DEPTH, LOCAL, 2 * SPECTRA), jnp.bfloat16),
+            dma((CHUNKS + 1,)),
             dma((2 * RINGS,)),
             dma((2 * RINGS,)),
             dma((3 * RINGS,)),
@@ -198,36 +228,40 @@
             dma,
         ],
         compiler_params=pltpu.CompilerParams(
-            collective_id=0, has_side_effects=True, vmem_limit_bytes=32 * 1024 * 1024
+            collective_id=0, has_side_effects=True, vmem_limit_bytes=56 * 1024 * 1024
         ),
         cost_estimate=pl.CostEstimate(flops=2 * 3 * 192 * 384 * 2048, bytes_accessed=6 << 20, transcendentals=1536),
         name="exchange",
-    )(volts, window, dft, mask)
-
-
-def correlate_kernel(rows, table, spectra, out):
-    first = pl.program_id(1) * rows
-    for r in range(rows):
-        a, b = table[first + r, 0], table[first + r, 1]
-        left = spectra[pl.ds(a * LOCAL, LOCAL), 0].reshape(BLOCK, 2 * SPECTRA)
-        right = spectra[pl.ds(b * LOCAL, LOCAL), 0].reshape(BLOCK, 2 * SPECTRA)
-        turned = jnp.concatenate([left[:, SPECTRA:], -left[:, :SPECTRA]], axis=1)
-        for part, lhs in ((0, left), (1, turned)):
-            vis = lax.dot_general(lhs, right, (((1,), (1,)), ((), ())), preferred_element_type=jnp.float32)
-            out[r, 0, part] = (vis * (1.0 / SPECTRA)).astype(jnp.bfloat16)
+    )(volts, table, mask)
+
+
+def correlate_kernel(table, spectra, out, vis, sem):
+    pairs = out.shape[0]
+
+    def pair(row, carry):
+        a, b = table[0, row], table[1, row]
+        for ch in range(DEPTH):
+            left = spectra[pl.ds(a * LOCAL, LOCAL), ch].reshape(BLOCK, 2 * SPECTRA)
+            right = spectra[pl.ds(b * LOCAL, LOCAL), ch].reshape(BLOCK, 2 * SPECTRA)
+            turned = jnp.concatenate([left[:, SPECTRA:], -left[:, :SPECTRA]], axis=1)
+            both = jnp.concatenate([left, turned], axis=0)
+            sums = lax.dot_general(both, right, (((1,), (1,)), ((), ())), preferred_element_type=jnp.float32)
+            vis[row, ch] = (sums * (1.0 / SPECTRA)).astype(jnp.bfloat16).reshape(2, BLOCK, BLOCK)
+        pltpu.make_async_copy(vis.at[row], out.at[row], sem).start()
+        return carry
+
+    lax.fori_loop(0, pairs, pair, 0, unroll=3)
+    pltpu.make_async_copy(vis, out, sem).wait()
 
 
 def correlate(table, spectra):
-    pairs, rows = table.shape[0], 3
+    shape = (table.shape[1], DEPTH, 2, BLOCK, BLOCK)
     return pl.pallas_call(
-        functools.partial(correlate_kernel, rows),
-        out_shape=jax.ShapeDtypeStruct((pairs, DEPTH, 2, BLOCK, BLOCK), jnp.bfloat16),
-        grid_spec=pltpu.PrefetchScalarGridSpec(
-            num_scalar_prefetch=1,
-            grid=(DEPTH, pairs // rows),
-            in_specs=[pl.BlockSpec((128, 1, LOCAL, 2 * SPECTRA), lambda ch, p, table: (0, ch, 0, 0))],
-            out_specs=pl.BlockSpec((rows, 1, 2, BLOCK, BLOCK), lambda ch, p, table: (p, ch, 0, 0, 0)),
-        ),
+        correlate_kernel,
+        out_shape=jax.ShapeDtypeStruct(shape, jnp.bfloat16),
+        in_specs=[pl.BlockSpec(memory_space=pltpu.SMEM), pl.BlockSpec(memory_space=pltpu.VMEM)],
+        out_specs=pl.BlockSpec(memory_space=pl.ANY),
+        scratch_shapes=[pltpu.VMEM(shape, jnp.bfloat16), pltpu.SemaphoreType.DMA],
         compiler_params=pltpu.CompilerParams(vmem_limit_bytes=32 * 1024 * 1024),
         cost_estimate=pl.CostEstimate(flops=2 * 54 * 256**3, bytes_accessed=10 << 20, transcendentals=0),
         name="correlate",
@@ -235,9 +269,8 @@
 
 
 def body(voltages, input_alive_mask, pair_table):
-    window, dft = tables()
-    spectra = exchange(voltages, jnp.asarray(window), jnp.asarray(dft), input_alive_mask.reshape(LOCAL, 1))
-    return correlate(pair_table, spectra)
+    spectra = exchange(voltages, jnp.asarray(tables()), input_alive_mask)
+    return correlate(pair_table.T, spectra)
 
 
 def solution(mesh):

time: 51.2 us -> 40.7 us (0.79)
  Pallas kernels: 46.3 us -> 40.5 us
  local copies, waits for them, and re-layouts: 4.62 us -> 0.01 us
    pallas_call x2, Pallas kernels: 46.3 us -> 40.5 us  [the longest x1 36.5 us: exchange(): pl.pallas_call(exchange_kernel, out_shape=pltpu.VMEM((128, DEPTH, LOCAL,...]
    unnamed x7 -> x2, local copies, waits for them, and re-layouts: 3.89 us -> 0.01 us
    reshape x1 -> x0, local copies, waits for them, and re-layouts: 0.73 us -> none  [body(): input_alive_mask.reshape(LOCAL, 1)]
where the time goes in v2:
time: 40.7 us; the launch traced here: 40.6 us
  Pallas kernels  40.5 us (100%)
    pallas_call x1, Pallas kernels, exchange(): pl.pallas_call(exchange_kernel, out_shape=pltpu.VMEM((128, DEPTH, LOCAL,...  36.5 us
    pallas_call x1, Pallas kernels, correlate(): pl.pallas_call(correlate_kernel, out_shape=jax.ShapeDtypeStruct(shape, jn...  4.02 us

profile of v2, /device:TPU:1, one launch (start us, length us, event | category | flops | bytes accessed | tf_op | source)
XLA Modules:
  0.0 40.6 jit_solution(12862246029206893392)
XLA Ops:
  0.0 0.0 copy-start
  0.0 36.5 %exchange.1.spectra = bf16[128,3,16,256]{3,2,1,0:T(8,128)(2,1)S(1)} custom-call(bf16[16,50304]{1,0:T(8,128)(2,1)} %volts_hbm.1, f32[392,384]{1,0:T(8,128)} %constant.2.clone.table_hbm, s32[16]{0:T(128)} %mask.1), custom_call_target="tpu_custom_call" | custom-call | flops 905969664 | bytes 6291456 | tf_op jit(solution)/shard_map/exchange/pallas_call | solution.py:208
  36.5 0.0 copy-done
  36.5 4.0 %correlate.1 = bf16[9,3,2,256,256]{4,3,2,1,0:T(8,128)(2,1)} custom-call(s32[2,9]{1,0:T(2,128)S(1)} %bitcast.1, bf16[128,3,16,256]{3,2,1,0:T(8,128)(2,1)S(1)} %exchange.1.spectra), custom_call_target="tpu_custom_call" | custom-call | flops 1811939328 | bytes 10485760 | tf_op jit(solution)/shard_map/correlate/pallas_call | solution.py:259
Async XLA Ops:
  0.0 36.5 %copy-start = (s32[9,2]{0,1:T(2,128)S(1)}, s32[9,2]{0,1:T(2,128)}, u32[]{:S(2)}) copy-start(s32[9,2]{0,1:T(2,128)} %param.6) | copy-start | bytes 220

commit v3 on v2

--- a/solution.py
+++ b/solution.py
@@ -21,10 +21,8 @@
 GROUPS = BAND // DEPTH
 MESH = pl.DeviceIdType.MESH
 
-ORDER = (
-    (1, 0), (0, 1), (3, 0), (0, 3), (2, 0), (0, 2), (1, 1), (3, 3),
-    (1, 3), (3, 1), (2, 1), (1, 2), (2, 3), (3, 2), (2, 2),
-)
+ORDER = ((0, 0), (0, 1), (0, 3), (1, 0), (1, 1), (1, 3), (0, 2), (1, 2))
+HALF = len(ORDER)
 
 
 def tables():
@@ -74,7 +72,7 @@
     return pl.ds(first * PERIOD, ((c + 1) * STEP + TAPS - 1 - first) * PERIOD)
 
 
-def channelize(volts_hbm, table_hbm, mask, volts, table, dft, fir, spec, ready, load):
+def channelize(volts_hbm, table_hbm, volts, table, dft, fir, spec, load, greet):
     loads = [pltpu.make_async_copy(table_hbm, table, load.at[CHUNKS])]
     for c in range(CHUNKS):
         loads.append(pltpu.make_async_copy(volts_hbm.at[:, chunk(c)], volts.at[:, chunk(c)], load.at[c]))
@@ -108,6 +106,8 @@
         loads[1 + c].wait()
         lax.fori_loop(c * STEP // 8, (c + 1) * STEP // 8, filt, 0, unroll=True)
 
+    greet(1)
+
     for pair in range(LOCAL // 2):
         highs, lows = [], []
         for i in (2 * pair, 2 * pair + 1):
@@ -121,46 +121,60 @@
         for half in range(2):
             spec[pl.ds(2 * pair + half, rows, stride=LOCAL), :] = out[:, half * SPECTRA : (half + 1) * SPECTRA]
 
+    greet(0)
+
+
+def equalize(ring, alive, spec, ready):
+    for e in range(2 * DEPTH):
+        at = pl.multiple_of((ring * 2 * DEPTH + e) * 2 * LOCAL, 2 * LOCAL)
+        re, im = spec[pl.ds(at, LOCAL), :], spec[pl.ds(at + LOCAL, LOCAL), :]
+        power = jnp.sum(re * re + im * im, axis=1, keepdims=True) * (1.0 / SPECTRA)
+        gain = lax.rsqrt(power + 1e-06) * alive
+        both = jnp.concatenate([re * gain, im * gain], axis=1)
+        ready[ring, e // DEPTH, e % DEPTH] = both.astype(jnp.bfloat16)
+
+
+def exchange_kernel(
+    volts_hbm, table_hbm, mask, out, volts, table, dft, fir, spec, ready, relay, load, s1, r1, s2, r2, s3, r3, sl
+):
+    z, x, y, c = place()
+    q, zc, zb = lax.rem(x, 2), lax.div(z, 2), lax.rem(z, 2)
+    other_core = device(z, x, y, 1 - c)
+    block = relay.at[0]
+    barrier = pltpu.get_barrier_semaphore()
+
+    def meet(f, j, sign):
+        a, dy = ORDER[j]
+        return lax.rem(zc + f, 2) * 2 + lax.rem(zb + a, 2), (ahead if sign > 0 else behind)(y, dy)
+
+    def signal(to):
+        pl.semaphore_signal(barrier, inc=1, device_id=to, device_id_type=MESH)
+
+    for j in range(1, HALF):
+        zd, yd = meet(0, j, 1)
+        signal(device(zd, x, yd, c))
+    for d in (1, 2, 3):
+        signal(device(z, ahead(x, d), y, c))
+    signal(other_core)
+
+    def greet(part):
+        @pl.when(zb == part)
+        def _():
+            pl.semaphore_wait(barrier, HALF + 3 + HALF * zc)
+            for j in range(HALF):
+                zd, yd = meet(1, j, 1)
+                signal(device(zd, x, yd, c))
+
+    channelize(volts_hbm, table_hbm, volts, table, dft, fir, spec, load, greet)
     inputs = lax.broadcasted_iota(jnp.int32, (LOCAL, 1), 0)
     alive = jnp.zeros((LOCAL, 1), jnp.float32)
     for i in range(LOCAL):
         alive = jnp.where(inputs == i, mask[i].astype(jnp.float32), alive)
 
-    def equalize(ring, carry):
-        for e in range(2 * DEPTH):
-            at = pl.multiple_of((ring * 2 * DEPTH + e) * 2 * LOCAL, 2 * LOCAL)
-            re, im = spec[pl.ds(at, LOCAL), :], spec[pl.ds(at + LOCAL, LOCAL), :]
-            power = jnp.sum(re * re + im * im, axis=1, keepdims=True) * (1.0 / SPECTRA)
-            gain = lax.rsqrt(power + 1e-06) * alive
-            both = jnp.concatenate([re * gain, im * gain], axis=1)
-            ready[ring, e // DEPTH, e % DEPTH] = both.astype(jnp.bfloat16)
-        return carry
-
-    lax.fori_loop(0, RINGS, equalize, 0, unroll=4)
-
-
-def exchange_kernel(
-    volts_hbm, table_hbm, mask, out, volts, table, dft, fir, spec, ready, relay, load, s1, r1, s2, r2, s3, r3, sl
-):
-    z, x, y, c = place()
-    q = lax.rem(x, 2)
-    barrier = pltpu.get_barrier_semaphore()
-    peers = [device(ahead(z, dz), x, ahead(y, dy), c) for dz, dy in ORDER]
-    peers += [device(z, ahead(x, d), y, c) for d in (1, 2, 3)] + [device(z, x, y, 1 - c)]
-    for peer in peers:
-        pl.semaphore_signal(barrier, inc=1, device_id=peer, device_id_type=MESH)
-
-    channelize(volts_hbm, table_hbm, mask, volts, table, dft, fir, spec, ready, load)
-
-    pl.semaphore_wait(barrier, len(peers))
-    sends = []
-
     def send(src, dst, send_sem, recv_sem, to):
-        copy = pltpu.make_async_remote_copy(
+        pltpu.make_async_remote_copy(
             src_ref=src, dst_ref=dst, send_sem=send_sem, recv_sem=recv_sem, device_id=to, device_id_type=MESH
-        )
-        copy.start()
-        sends.append(copy)
+        ).start()
 
     def arrived(dst, sem):
         pltpu.make_async_copy(dst, dst, sem).wait()
@@ -170,35 +184,81 @@
         send(others, out.at[at], s2.at[3 * k + 1], r2.at[3 * k + 1], device(z, ahead(x, 1), y, c))
         send(others, out.at[at], s2.at[3 * k + 2], r2.at[3 * k + 2], device(z, ahead(x, 3), y, c))
         send(mine, out.at[at], s2.at[3 * k], r2.at[3 * k], device(z, ahead(x, 2), y, c))
-        send(mine, out.at[at], s3.at[4 * k], r3.at[4 * k], device(z, x, y, 1 - c))
+        send(mine, out.at[at], s3.at[4 * k], r3.at[4 * k], other_core)
 
     here, own = z * SIDE + y, slot(z, x, y, c)
-    spread(0, z, y, ready.at[here, q], ready.at[here, 1 - q])
-    keep = pltpu.make_async_copy(ready.at[here, q], out.at[own], sl)
-    keep.start()
-    for k, (dz, dy) in enumerate(ORDER, 1):
-        zd, yd = ahead(z, dz), ahead(y, dy)
+
+    def depart(f, j):
+        k = f * HALF + j
+        zd, yd = meet(f, j, 1)
         to, there = device(zd, x, yd, c), zd * SIDE + yd
         send(ready.at[there, 1 - q], relay.at[here], s1.at[2 * k + 1], r1.at[2 * k + 1], to)
         send(ready.at[there, q], out.at[own], s1.at[2 * k], r1.at[2 * k], to)
-    for k, (dz, dy) in enumerate(ORDER, 1):
-        zs, ys = behind(z, dz), behind(y, dy)
+
+    def relay_on(f, j):
+        k = f * HALF + j
+        zs, ys = meet(f, j, -1)
         at, ring = slot(zs, x, ys, c), zs * SIDE + ys
         arrived(relay.at[ring], r1.at[2 * k + 1])
         arrived(out.at[at], r1.at[2 * k])
         spread(k, zs, ys, out.at[at], relay.at[ring])
-    for k, (dz, dy) in enumerate(((0, 0),) + ORDER):
-        zs, ys = behind(z, dz), behind(y, dy)
-        for j, d in ((1, 1), (2, 3), (0, 2)):
+
+    def hand_over(f, j):
+        k = f * HALF + j
+        zs, ys = meet(f, j, -1)
+        for i, d in ((1, 1), (2, 3), (0, 2)):
             at = slot(zs, behind(x, d), ys, c)
-            arrived(out.at[at], r2.at[3 * k + j])
-            send(out.at[at], out.at[at], s3.at[4 * k + 1 + j], r3.at[4 * k + 1 + j], device(z, x, y, 1 - c))
-    for k, (dz, dy) in enumerate(((0, 0),) + ORDER):
-        zs, ys = behind(z, dz), behind(y, dy)
-        for j, d in ((-1, 0), (1, 1), (2, 3), (0, 2)):
-            arrived(out.at[slot(zs, behind(x, d), ys, 1 - c)], r3.at[4 * k + 1 + j])
-    for copy in sends:
-        copy.wait_send()
+            arrived(out.at[at], r2.at[3 * k + i])
+            send(out.at[at], out.at[at], s3.at[4 * k + 1 + i], r3.at[4 * k + 1 + i], other_core)
+
+    for j in range(HALF):
+        zd, yd = meet(0, j, 1)
+        equalize(zd * SIDE + yd, alive, spec, ready)
+        if j == 0:
+            spread(0, z, y, ready.at[here, q], ready.at[here, 1 - q])
+            keep = pltpu.make_async_copy(ready.at[here, q], out.at[own], sl)
+            keep.start()
+        elif j == 3 or j == 7:
+            for earlier in range(max(1, j - 3), j + 1):
+                depart(0, earlier)
+    for j in range(HALF):
+        zd, yd = meet(1, j, 1)
+        equalize(zd * SIDE + yd, alive, spec, ready)
+
+    @pl.when(zc == 0)
+    def _():
+        for j in range(1, HALF):
+            relay_on(0, j)
+        pl.semaphore_wait(barrier, HALF)
+
+    for j in range(HALF):
+        depart(1, j)
+
+    @pl.when(zc == 1)
+    def _():
+        for j in range(HALF):
+            relay_on(1, j)
+
+    for j in range(HALF):
+        hand_over(zc, j)
+        if j == 0:
+            pl.when(zc == 0)(lambda: relay_on(1, 0))
+        else:
+            relay_on(1 - zc, j)
+    for j in range(HALF):
+        hand_over(1 - zc, j)
+
+    def finish(sems, first, count):
+        def one(i, carry):
+            arrived(block, sems.at[i])
+            return carry
+
+        lax.fori_loop(first, count, one, 0)
+
+    finish(r3, 0, 4 * RINGS)
+    finish(s1, 2, 2 * RINGS)
+    finish(s2, 0, 3 * RINGS)
+    finish(s3, 0, 4 * RINGS)
     keep.wait()
 
 

time: 40.7 us -> 49.9 us (1.23)
  the two profiles are of different devices: /device:TPU:1 before, /device:TPU:65 now
where the time goes in v3:
time: 49.9 us; the launch traced here: 49.8 us
  Pallas kernels  49.7 us (100%)
    pallas_call x1, Pallas kernels, exchange(): pl.pallas_call(exchange_kernel, out_shape=pltpu.VMEM((128, DEPTH, LOCAL,...  45.7 us
    pallas_call x1, Pallas kernels, correlate(): pl.pallas_call(correlate_kernel, out_shape=jax.ShapeDtypeStruct(shape, jn...  4.02 us

profile of v3, /device:TPU:65, one launch (start us, length us, event | category | flops | bytes accessed | tf_op | source)
XLA Modules:
  0.0 49.8 jit_solution(17653866198312752286)
XLA Ops:
  0.0 0.0 copy-start
  0.0 45.7 %exchange.1.spectra = bf16[128,3,16,256]{3,2,1,0:T(8,128)(2,1)S(1)} custom-call(bf16[16,50304]{1,0:T(8,128)(2,1)} %volts_hbm.1, f32[392,384]{1,0:T(8,128)} %constant.2.clone.table_hbm, s32[16]{0:T(128)} %mask.1), custom_call_target="tpu_custom_call" | custom-call | flops 905969664 | bytes 6291456 | tf_op jit(solution)/shard_map/exchange/pallas_call | solution.py:268
  45.7 0.0 copy-done
  45.7 4.0 %correlate.1 = bf16[9,3,2,256,256]{4,3,2,1,0:T(8,128)(2,1)} custom-call(s32[2,9]{1,0:T(2,128)S(1)} %bitcast.1, bf16[128,3,16,256]{3,2,1,0:T(8,128)(2,1)S(1)} %exchange.1.spectra), custom_call_target="tpu_custom_call" | custom-call | flops 1811939328 | bytes 10485760 | tf_op jit(solution)/shard_map/correlate/pallas_call | solution.py:319
Async XLA Ops:
  0.0 45.7 %copy-start = (s32[9,2]{0,1:T(2,128)S(1)}, s32[9,2]{0,1:T(2,128)}, u32[]{:S(2)}) copy-start(s32[9,2]{0,1:T(2,128)} %param.6) | copy-start | bytes 220

commit v4 on v2

--- a/solution.py
+++ b/solution.py
@@ -22,9 +22,12 @@
 MESH = pl.DeviceIdType.MESH
 
 ORDER = (
-    (1, 0), (0, 1), (3, 0), (0, 3), (2, 0), (0, 2), (1, 1), (3, 3),
-    (1, 3), (3, 1), (2, 1), (1, 2), (2, 3), (3, 2), (2, 2),
+    (0, 1), (3, 0), (0, 3), (3, 1), (0, 2), (3, 3), (2, 0), (3, 2),
+    (2, 1), (1, 0), (2, 3), (1, 1), (2, 2), (1, 3), (1, 2),
 )
+
+
+PLANES = (0, 3, 2, 1)
 
 
 def tables():
@@ -74,7 +77,7 @@
     return pl.ds(first * PERIOD, ((c + 1) * STEP + TAPS - 1 - first) * PERIOD)
 
 
-def channelize(volts_hbm, table_hbm, mask, volts, table, dft, fir, spec, ready, load):
+def channelize(volts_hbm, table_hbm, volts, table, dft, fir, spec, load):
     loads = [pltpu.make_async_copy(table_hbm, table, load.at[CHUNKS])]
     for c in range(CHUNKS):
         loads.append(pltpu.make_async_copy(volts_hbm.at[:, chunk(c)], volts.at[:, chunk(c)], load.at[c]))
@@ -121,84 +124,96 @@
         for half in range(2):
             spec[pl.ds(2 * pair + half, rows, stride=LOCAL), :] = out[:, half * SPECTRA : (half + 1) * SPECTRA]
 
+
+def equalize(ring, alive, spec, ready):
+    for e in range(2 * DEPTH):
+        at = pl.multiple_of((ring * 2 * DEPTH + e) * 2 * LOCAL, 2 * LOCAL)
+        re, im = spec[pl.ds(at, LOCAL), :], spec[pl.ds(at + LOCAL, LOCAL), :]
+        power = jnp.sum(re * re + im * im, axis=1, keepdims=True) * (1.0 / SPECTRA)
+        gain = lax.rsqrt(power + 1e-06) * alive
+        both = jnp.concatenate([re * gain, im * gain], axis=1)
+        ready[ring, e // DEPTH, e % DEPTH] = both.astype(jnp.bfloat16)
+
+
+def exchange_kernel(
+    volts_hbm, table_hbm, mask_hbm, out, volts, table, mask, dft, fir, spec, ready, relay, load, s1, s2, s3, r1, r2, r3, sl
+):
+    z, x, y, c = place()
+    q = lax.rem(x, 2)
+    here, own = z * SIDE + y, slot(z, x, y, c)
+    other_core = device(z, x, y, 1 - c)
+    barrier = pltpu.get_barrier_semaphore()
+    peers = [device(ahead(z, dz), x, ahead(y, dy), c) for dz, dy in ORDER]
+    peers += [device(z, ahead(x, d), y, c) for d in (1, 2, 3)] + [other_core]
+    for peer in peers:
+        pl.semaphore_signal(barrier, inc=1, device_id=peer, device_id_type=MESH)
+
+    alive_load = pltpu.make_async_copy(mask_hbm, mask, load.at[CHUNKS + 1])
+    alive_load.start()
+    channelize(volts_hbm, table_hbm, volts, table, dft, fir, spec, load)
+    alive_load.wait()
     inputs = lax.broadcasted_iota(jnp.int32, (LOCAL, 1), 0)
     alive = jnp.zeros((LOCAL, 1), jnp.float32)
     for i in range(LOCAL):
         alive = jnp.where(inputs == i, mask[i].astype(jnp.float32), alive)
 
-    def equalize(ring, carry):
-        for e in range(2 * DEPTH):
-            at = pl.multiple_of((ring * 2 * DEPTH + e) * 2 * LOCAL, 2 * LOCAL)
-            re, im = spec[pl.ds(at, LOCAL), :], spec[pl.ds(at + LOCAL, LOCAL), :]
-            power = jnp.sum(re * re + im * im, axis=1, keepdims=True) * (1.0 / SPECTRA)
-            gain = lax.rsqrt(power + 1e-06) * alive
-            both = jnp.concatenate([re * gain, im * gain], axis=1)
-            ready[ring, e // DEPTH, e % DEPTH] = both.astype(jnp.bfloat16)
-        return carry
-
-    lax.fori_loop(0, RINGS, equalize, 0, unroll=4)
-
-
-def exchange_kernel(
-    volts_hbm, table_hbm, mask, out, volts, table, dft, fir, spec, ready, relay, load, s1, r1, s2, r2, s3, r3, sl
-):
-    z, x, y, c = place()
-    q = lax.rem(x, 2)
-    barrier = pltpu.get_barrier_semaphore()
-    peers = [device(ahead(z, dz), x, ahead(y, dy), c) for dz, dy in ORDER]
-    peers += [device(z, ahead(x, d), y, c) for d in (1, 2, 3)] + [device(z, x, y, 1 - c)]
-    for peer in peers:
-        pl.semaphore_signal(barrier, inc=1, device_id=peer, device_id_type=MESH)
-
-    channelize(volts_hbm, table_hbm, mask, volts, table, dft, fir, spec, ready, load)
-
+    def send(src, dst, send_sem, recv_sem, to):
+        pltpu.make_async_remote_copy(
+            src_ref=src, dst_ref=dst, send_sem=send_sem, recv_sem=recv_sem, device_id=to, device_id_type=MESH
+        ).start()
+
+    def arrived(blocks, sem):
+        pltpu.make_async_copy(blocks, blocks, sem).wait()
+
+    def spread(ring, at, mine, others):
+        send(others, out.at[at], s2, r2.at[ring], device(z, ahead(x, 1), y, c))
+        send(others, out.at[at], s2, r2.at[ring], device(z, ahead(x, 3), y, c))
+        send(mine, out.at[at], s2, r2.at[ring], device(z, ahead(x, 2), y, c))
+        send(mine, out.at[at], s3, r3, other_core)
+
+    def depart(dz, dy):
+        zd, yd = ahead(z, dz), ahead(y, dy)
+        to, there = device(zd, x, yd, c), zd * SIDE + yd
+        send(ready.at[there, 1 - q], relay.at[here], s1, r1.at[here], to)
+        send(ready.at[there, q], out.at[own], s1, r1.at[here], to)
+
+    def relay_on(dz):
+        zs = behind(z, dz)
+        for dy in range(SIDE):
+            ys = behind(y, dy)
+            ring, at = zs * SIDE + ys, slot(zs, x, ys, c)
+            if (dz, dy) != (0, 0):
+                arrived(relay.at[pl.ds(0, 2)], r1.at[ring])
+                spread(ring, at, out.at[at], relay.at[ring])
+
+    def hand_over(dz):
+        zs = behind(z, dz)
+        for dy in range(SIDE):
+            ys = behind(y, dy)
+            arrived(relay.at[pl.ds(0, 3)], r2.at[zs * SIDE + ys])
+            for d in (1, 3, 2):
+                at = slot(zs, behind(x, d), ys, c)
+                send(out.at[at], out.at[at], s3, r3, other_core)
+
+    equalize(here, alive, spec, ready)
     pl.semaphore_wait(barrier, len(peers))
-    sends = []
-
-    def send(src, dst, send_sem, recv_sem, to):
-        copy = pltpu.make_async_remote_copy(
-            src_ref=src, dst_ref=dst, send_sem=send_sem, recv_sem=recv_sem, device_id=to, device_id_type=MESH
-        )
-        copy.start()
-        sends.append(copy)
-
-    def arrived(dst, sem):
-        pltpu.make_async_copy(dst, dst, sem).wait()
-
-    def spread(k, zs, ys, mine, others):
-        at = slot(zs, x, ys, c)
-        send(others, out.at[at], s2.at[3 * k + 1], r2.at[3 * k + 1], device(z, ahead(x, 1), y, c))
-        send(others, out.at[at], s2.at[3 * k + 2], r2.at[3 * k + 2], device(z, ahead(x, 3), y, c))
-        send(mine, out.at[at], s2.at[3 * k], r2.at[3 * k], device(z, ahead(x, 2), y, c))
-        send(mine, out.at[at], s3.at[4 * k], r3.at[4 * k], device(z, x, y, 1 - c))
-
-    here, own = z * SIDE + y, slot(z, x, y, c)
-    spread(0, z, y, ready.at[here, q], ready.at[here, 1 - q])
+    spread(here, own, ready.at[here, q], ready.at[here, 1 - q])
     keep = pltpu.make_async_copy(ready.at[here, q], out.at[own], sl)
     keep.start()
-    for k, (dz, dy) in enumerate(ORDER, 1):
-        zd, yd = ahead(z, dz), ahead(y, dy)
-        to, there = device(zd, x, yd, c), zd * SIDE + yd
-        send(ready.at[there, 1 - q], relay.at[here], s1.at[2 * k + 1], r1.at[2 * k + 1], to)
-        send(ready.at[there, q], out.at[own], s1.at[2 * k], r1.at[2 * k], to)
-    for k, (dz, dy) in enumerate(ORDER, 1):
-        zs, ys = behind(z, dz), behind(y, dy)
-        at, ring = slot(zs, x, ys, c), zs * SIDE + ys
-        arrived(relay.at[ring], r1.at[2 * k + 1])
-        arrived(out.at[at], r1.at[2 * k])
-        spread(k, zs, ys, out.at[at], relay.at[ring])
-    for k, (dz, dy) in enumerate(((0, 0),) + ORDER):
-        zs, ys = behind(z, dz), behind(y, dy)
-        for j, d in ((1, 1), (2, 3), (0, 2)):
-            at = slot(zs, behind(x, d), ys, c)
-            arrived(out.at[at], r2.at[3 * k + j])
-            send(out.at[at], out.at[at], s3.at[4 * k + 1 + j], r3.at[4 * k + 1 + j], device(z, x, y, 1 - c))
-    for k, (dz, dy) in enumerate(((0, 0),) + ORDER):
-        zs, ys = behind(z, dz), behind(y, dy)
-        for j, d in ((-1, 0), (1, 1), (2, 3), (0, 2)):
-            arrived(out.at[slot(zs, behind(x, d), ys, 1 - c)], r3.at[4 * k + 1 + j])
-    for copy in sends:
-        copy.wait_send()
+    for first in range(0, len(ORDER), 3):
+        for dz, dy in ORDER[first : first + 3]:
+            equalize(ahead(z, dz) * SIDE + ahead(y, dy), alive, spec, ready)
+        for dz, dy in ORDER[first : first + 3]:
+            depart(dz, dy)
+    relay_on(PLANES[0])
+    for last, dz in zip(PLANES, PLANES[1:]):
+        relay_on(dz)
+    for dz in PLANES:
+        hand_over(dz)
+    arrived(out.at[pl.ds(0, 4 * RINGS)], r3)
+    arrived(ready.at[pl.ds(0, RINGS - 1)], s1)
+    arrived(out.at[pl.ds(0, 3 * RINGS)], s2)
+    arrived(out.at[pl.ds(0, 4 * RINGS)], s3)
     keep.wait()
 
 
@@ -208,23 +223,24 @@
     return pl.pallas_call(
         exchange_kernel,
         out_shape=pltpu.VMEM((128, DEPTH, LOCAL, 2 * SPECTRA), jnp.bfloat16),
-        in_specs=[anywhere, anywhere, pl.BlockSpec(memory_space=pltpu.SMEM)],
+        in_specs=[anywhere] * 3,
         out_specs=pl.BlockSpec(memory_space=pl.ANY),
         scratch_shapes=[
             pltpu.VMEM(volts.shape, jnp.bfloat16),
             pltpu.VMEM(table.shape, jnp.float32),
+            pltpu.SMEM(mask.shape, jnp.int32),
             pltpu.VMEM((2 * BAND, 3 * PERIOD), jnp.bfloat16),
             pltpu.VMEM((3, SPECTRA * PITCH, 128), jnp.float32),
             pltpu.VMEM((2 * BAND * LOCAL, SPECTRA), jnp.float32),
             pltpu.VMEM((RINGS, 2, DEPTH, LOCAL, 2 * SPECTRA), jnp.bfloat16),
             pltpu.VMEM((RINGS, DEPTH, LOCAL, 2 * SPECTRA), jnp.bfloat16),
-            dma((CHUNKS + 1,)),
-            dma((2 * RINGS,)),
-            dma((2 * RINGS,)),
-            dma((3 * RINGS,)),
-            dma((3 * RINGS,)),
-            dma((4 * RINGS,)),
-            dma((4 * RINGS,)),
+            dma((CHUNKS + 2,)),
+            dma,
+            dma,
+            dma,
+            dma((RINGS,)),
+            dma((RINGS,)),
+            dma,
             dma,
         ],
         compiler_params=pltpu.CompilerParams(

time: 40.7 us -> 36.7 us (0.902)
  Pallas kernels: 40.5 us -> 36.6 us
    pallas_call x1, Pallas kernels: 36.5 us -> 32.5 us  [exchange(): pl.pallas_call(exchange_kernel, out_shape=pltpu.VMEM((128, DEPTH, LOCAL,...]
where the time goes in v4:
time: 36.7 us; the launch traced here: 36.6 us
  Pallas kernels  36.6 us (100%)
    pallas_call x1, Pallas kernels, exchange(): pl.pallas_call(exchange_kernel, out_shape=pltpu.VMEM((128, DEPTH, LOCAL,...  32.5 us
    pallas_call x1, Pallas kernels, correlate(): pl.pallas_call(correlate_kernel, out_shape=jax.ShapeDtypeStruct(shape, jn...  4.01 us

profile of v4, /device:TPU:1, one launch (start us, length us, event | category | flops | bytes accessed | tf_op | source)
XLA Modules:
  0.0 36.6 jit_solution(11404054723656558484)
XLA Ops:
  0.0 0.0 copy-start
  0.0 32.5 %exchange.1.spectra = bf16[128,3,16,256]{3,2,1,0:T(8,128)(2,1)S(1)} custom-call(bf16[16,50304]{1,0:T(8,128)(2,1)} %volts_hbm.1, f32[392,384]{1,0:T(8,128)} %constant.2.clone.table_hbm, s32[16]{0:T(128)} %mask_hbm.1), custom_call_target="tpu_custom_call" | custom-call | flops 905969664 | bytes 6291456 | tf_op jit(solution)/shard_map/exchange/pallas_call | solution.py:223
  32.6 0.0 copy-done
  32.6 4.0 %correlate.1 = bf16[9,3,2,256,256]{4,3,2,1,0:T(8,128)(2,1)} custom-call(s32[2,9]{1,0:T(2,128)S(1)} %bitcast.1, bf16[128,3,16,256]{3,2,1,0:T(8,128)(2,1)S(1)} %exchange.1.spectra), custom_call_target="tpu_custom_call" | custom-call | flops 1811939328 | bytes 10485760 | tf_op jit(solution)/shard_map/correlate/pallas_call | solution.py:275
Async XLA Ops:
  0.0 32.6 %copy-start = (s32[9,2]{0,1:T(2,128)S(1)}, s32[9,2]{0,1:T(2,128)}, u32[]{:S(2)}) copy-start(s32[9,2]{0,1:T(2,128)} %param.6) | copy-start | bytes 220

commit v5 on v4

--- a/solution.py
+++ b/solution.py
@@ -21,13 +21,7 @@
 GROUPS = BAND // DEPTH
 MESH = pl.DeviceIdType.MESH
 
-ORDER = (
-    (0, 1), (3, 0), (0, 3), (3, 1), (0, 2), (3, 3), (2, 0), (3, 2),
-    (2, 1), (1, 0), (2, 3), (1, 1), (2, 2), (1, 3), (1, 2),
-)
-
-
-PLANES = (0, 3, 2, 1)
+NEAR = (1, 3, 2)
 
 
 def tables():
@@ -77,7 +71,7 @@
     return pl.ds(first * PERIOD, ((c + 1) * STEP + TAPS - 1 - first) * PERIOD)
 
 
-def channelize(volts_hbm, table_hbm, volts, table, dft, fir, spec, load):
+def channelize(volts_hbm, table_hbm, volts, table, dft, fir, spec, load, between):
     loads = [pltpu.make_async_copy(table_hbm, table, load.at[CHUNKS])]
     for c in range(CHUNKS):
         loads.append(pltpu.make_async_copy(volts_hbm.at[:, chunk(c)], volts.at[:, chunk(c)], load.at[c]))
@@ -87,9 +81,9 @@
         part.start()
     loads[0].wait()
     rows = 2 * BAND
-    dft[:, 0:PERIOD] = table[0:rows].astype(jnp.bfloat16)
-    dft[:, PERIOD : 2 * PERIOD] = table[rows : 2 * rows].astype(jnp.bfloat16)
-    dft[:, 2 * PERIOD :] = dft[:, 0:PERIOD]
+    parts = table[0 : 2 * rows].astype(jnp.bfloat16)
+    dft[:, 0:PERIOD] = parts
+    dft[:, PERIOD:] = parts
 
     def filt(step, carry):
         first = step * 8
@@ -111,6 +105,7 @@
         loads[1 + c].wait()
         lax.fori_loop(c * STEP // 8, (c + 1) * STEP // 8, filt, 0, unroll=True)
 
+    between()
     for pair in range(LOCAL // 2):
         highs, lows = [], []
         for i in (2 * pair, 2 * pair + 1):
@@ -119,8 +114,9 @@
             highs.append(high)
             lows.append((x - high.astype(jnp.float32)).astype(jnp.bfloat16))
         high, low = jnp.concatenate(highs, axis=0), jnp.concatenate(lows, axis=0)
-        right = jnp.concatenate([high, high, low], axis=1)
-        out = lax.dot_general(dft[...], right, (((1,), (1,)), ((), ())), preferred_element_type=jnp.float32)
+        right = jnp.concatenate([high, low], axis=1)
+        both = lax.dot_general(dft[...], right, (((1,), (1,)), ((), ())), preferred_element_type=jnp.float32)
+        out = both[:rows] + both[rows:]
         for half in range(2):
             spec[pl.ds(2 * pair + half, rows, stride=LOCAL), :] = out[:, half * SPECTRA : (half + 1) * SPECTRA]
 
@@ -136,21 +132,48 @@
 
 
 def exchange_kernel(
-    volts_hbm, table_hbm, mask_hbm, out, volts, table, mask, dft, fir, spec, ready, relay, load, s1, s2, s3, r1, r2, r3, sl
+    volts_hbm, table_hbm, mask_hbm, pairs_hbm, out, pairs, volts, table, mask, dft, fir, spec, ready, relay, load, s1, s2, s3, r1, r2, r3, sl
 ):
     z, x, y, c = place()
     q = lax.rem(x, 2)
     here, own = z * SIDE + y, slot(z, x, y, c)
     other_core = device(z, x, y, 1 - c)
     barrier = pltpu.get_barrier_semaphore()
-    peers = [device(ahead(z, dz), x, ahead(y, dy), c) for dz, dy in ORDER]
-    peers += [device(z, ahead(x, d), y, c) for d in (1, 2, 3)] + [other_core]
-    for peer in peers:
-        pl.semaphore_signal(barrier, inc=1, device_id=peer, device_id_type=MESH)
+
+    def signal(to):
+        pl.semaphore_signal(barrier, inc=1, device_id=to, device_id_type=MESH)
+
+    def plane(zd):
+        for dy in range(SIDE):
+            signal(device(zd, x, ahead(y, dy), c))
+
+    for dy in NEAR:
+        signal(device(z, x, ahead(y, dy), c))
+    for d in (1, 2, 3):
+        signal(device(z, ahead(x, d), y, c))
+    signal(other_core)
+    for dz in (1, 2, 3):
+        pl.when((z > 0) & (ahead(z, dz) > 0))(lambda dz=dz: plane(ahead(z, dz)))
+
+    def greet_first():
+        pl.semaphore_wait(barrier, 7)
+        for zd in (1, 2, 3):
+            plane(zd)
+
+    def greet_others():
+        pl.semaphore_wait(barrier, 7 + 3 * SIDE)
+        plane(0)
+
+    def between():
+        pl.when(z == 0)(greet_first)
+        pl.when(z == 3)(greet_others)
 
     alive_load = pltpu.make_async_copy(mask_hbm, mask, load.at[CHUNKS + 1])
     alive_load.start()
-    channelize(volts_hbm, table_hbm, volts, table, dft, fir, spec, load)
+    pairs_load = pltpu.make_async_copy(pairs_hbm, pairs, load.at[CHUNKS + 2])
+    pairs_load.start()
+    channelize(volts_hbm, table_hbm, volts, table, dft, fir, spec, load, between)
+    pl.when((z == 1) | (z == 2))(greet_others)
     alive_load.wait()
     inputs = lax.broadcasted_iota(jnp.int32, (LOCAL, 1), 0)
     alive = jnp.zeros((LOCAL, 1), jnp.float32)
@@ -171,24 +194,26 @@
         send(mine, out.at[at], s2, r2.at[ring], device(z, ahead(x, 2), y, c))
         send(mine, out.at[at], s3, r3, other_core)
 
-    def depart(dz, dy):
-        zd, yd = ahead(z, dz), ahead(y, dy)
-        to, there = device(zd, x, yd, c), zd * SIDE + yd
-        send(ready.at[there, 1 - q], relay.at[here], s1, r1.at[here], to)
-        send(ready.at[there, q], out.at[own], s1, r1.at[here], to)
-
-    def relay_on(dz):
-        zs = behind(z, dz)
-        for dy in range(SIDE):
+    def prepare(dz):
+        for dy in ((0,) if dz else ()) + NEAR:
+            equalize(ahead(z, dz) * SIDE + ahead(y, dy), alive, spec, ready)
+
+    def depart(zd, offsets=(0,) + NEAR):
+        for dy in offsets:
+            yd = ahead(y, dy)
+            to, there = device(zd, x, yd, c), zd * SIDE + yd
+            send(ready.at[there, 1 - q], relay.at[here], s1, r1.at[here], to)
+            send(ready.at[there, q], out.at[own], s1, r1.at[here], to)
+
+    def relay_on(zs, offsets=(0,) + NEAR):
+        for dy in offsets:
             ys = behind(y, dy)
             ring, at = zs * SIDE + ys, slot(zs, x, ys, c)
-            if (dz, dy) != (0, 0):
-                arrived(relay.at[pl.ds(0, 2)], r1.at[ring])
-                spread(ring, at, out.at[at], relay.at[ring])
-
-    def hand_over(dz):
-        zs = behind(z, dz)
-        for dy in range(SIDE):
+            arrived(relay.at[pl.ds(0, 2)], r1.at[ring])
+            spread(ring, at, out.at[at], relay.at[ring])
+
+    def hand_over(zs):
+        for dy in (0,) + NEAR:
             ys = behind(y, dy)
             arrived(relay.at[pl.ds(0, 3)], r2.at[zs * SIDE + ys])
             for d in (1, 3, 2):
@@ -196,45 +221,62 @@
                 send(out.at[at], out.at[at], s3, r3, other_core)
 
     equalize(here, alive, spec, ready)
-    pl.semaphore_wait(barrier, len(peers))
     spread(here, own, ready.at[here, q], ready.at[here, 1 - q])
     keep = pltpu.make_async_copy(ready.at[here, q], out.at[own], sl)
     keep.start()
-    for first in range(0, len(ORDER), 3):
-        for dz, dy in ORDER[first : first + 3]:
-            equalize(ahead(z, dz) * SIDE + ahead(y, dy), alive, spec, ready)
-        for dz, dy in ORDER[first : first + 3]:
-            depart(dz, dy)
-    relay_on(PLANES[0])
-    for last, dz in zip(PLANES, PLANES[1:]):
-        relay_on(dz)
-    for dz in PLANES:
-        hand_over(dz)
+    late = lax.div(z, 3)
+    order = [behind(z, dz) for dz in (3 - late, 2 - late, 1 + 2 * late)]
+    prepare(0)
+    depart(z, NEAR)
+    for dz in (3, 2, 1):
+        prepare(dz)
+
+    @pl.when(z > 0)
+    def _():
+        for dz in (3, 2, 1):
+            depart(ahead(z, dz))
+
+    relay_on(z, NEAR)
+
+    @pl.when(z == 0)
+    def _():
+        pl.semaphore_wait(barrier, 3 * SIDE)
+        for zd in (3, 2, 1):
+            depart(zd)
+
+    for zs in order:
+        relay_on(zs)
+    for zs in [z] + order:
+        hand_over(zs)
     arrived(out.at[pl.ds(0, 4 * RINGS)], r3)
     arrived(ready.at[pl.ds(0, RINGS - 1)], s1)
     arrived(out.at[pl.ds(0, 3 * RINGS)], s2)
     arrived(out.at[pl.ds(0, 4 * RINGS)], s3)
     keep.wait()
-
-
-def exchange(volts, table, mask):
+    pairs_load.wait()
+
+
+def exchange(volts, table, mask, pairs):
     dma = pltpu.SemaphoreType.DMA
     anywhere = pl.BlockSpec(memory_space=pltpu.HBM)
     return pl.pallas_call(
         exchange_kernel,
-        out_shape=pltpu.VMEM((128, DEPTH, LOCAL, 2 * SPECTRA), jnp.bfloat16),
-        in_specs=[anywhere] * 3,
-        out_specs=pl.BlockSpec(memory_space=pl.ANY),
+        out_shape=(
+            pltpu.VMEM((128, DEPTH, LOCAL, 2 * SPECTRA), jnp.bfloat16),
+            pltpu.SMEM(pairs.shape, pairs.dtype),
+        ),
+        in_specs=[anywhere] * 4,
+        out_specs=(pl.BlockSpec(memory_space=pl.ANY), pl.BlockSpec(memory_space=pl.ANY)),
         scratch_shapes=[
             pltpu.VMEM(volts.shape, jnp.bfloat16),
             pltpu.VMEM(table.shape, jnp.float32),
             pltpu.SMEM(mask.shape, jnp.int32),
-            pltpu.VMEM((2 * BAND, 3 * PERIOD), jnp.bfloat16),
+            pltpu.VMEM((4 * BAND, 2 * PERIOD), jnp.bfloat16),
             pltpu.VMEM((3, SPECTRA * PITCH, 128), jnp.float32),
             pltpu.VMEM((2 * BAND * LOCAL, SPECTRA), jnp.float32),
             pltpu.VMEM((RINGS, 2, DEPTH, LOCAL, 2 * SPECTRA), jnp.bfloat16),
             pltpu.VMEM((RINGS, DEPTH, LOCAL, 2 * SPECTRA), jnp.bfloat16),
-            dma((CHUNKS + 2,)),
+            dma((CHUNKS + 3,)),
             dma,
             dma,
             dma,
@@ -248,7 +290,7 @@
         ),
         cost_estimate=pl.CostEstimate(flops=2 * 3 * 192 * 384 * 2048, bytes_accessed=6 << 20, transcendentals=1536),
         name="exchange",
-    )(volts, table, mask)
+    )(volts, table, mask, pairs)
 
 
 def correlate_kernel(table, spectra, out, vis, sem):
@@ -263,10 +305,10 @@
             both = jnp.concatenate([left, turned], axis=0)
             sums = lax.dot_general(both, right, (((1,), (1,)), ((), ())), preferred_element_type=jnp.float32)
             vis[row, ch] = (sums * (1.0 / SPECTRA)).astype(jnp.bfloat16).reshape(2, BLOCK, BLOCK)
-        pltpu.make_async_copy(vis.at[row], out.at[row], sem).start()
+            pltpu.make_async_copy(vis.at[row, ch], out.at[row, ch], sem).start()
         return carry
 
-    lax.fori_loop(0, pairs, pair, 0, unroll=3)
+    lax.fori_loop(0, pairs, pair, 0, unroll=True)
     pltpu.make_async_copy(vis, out, sem).wait()
 
 
@@ -285,8 +327,8 @@
 
 
 def body(voltages, input_alive_mask, pair_table):
-    spectra = exchange(voltages, jnp.asarray(tables()), input_alive_mask)
-    return correlate(pair_table.T, spectra)
+    spectra, pairs = exchange(voltages, jnp.asarray(tables()), input_alive_mask, pair_table.T)
+    return correlate(pairs, spectra)
 
 
 def solution(mesh):

time: 36.7 us -> 35.3 us (0.962)
  the two profiles are of different devices: /device:TPU:1 before, /device:TPU:97 now
where the time goes in v5:
time: 35.3 us; the launch traced here: 35.2 us
  Pallas kernels  35.2 us (100%)
    pallas_call x1, Pallas kernels, exchange(): pl.pallas_call(exchange_kernel, out_shape=(pltpu.VMEM((128, DEPTH, LOCAL,...  32 us
    pallas_call x1, Pallas kernels, correlate(): pl.pallas_call(correlate_kernel, out_shape=jax.ShapeDtypeStruct(shape, jn...  3.19 us

profile of v5, /device:TPU:97, one launch (start us, length us, event | category | flops | bytes accessed | tf_op | source)
XLA Modules:
  0.0 35.2 jit_solution(7664514758512815251)
XLA Ops:
  0.0 32.0 %exchange.1 = (bf16[128,3,16,256]{3,2,1,0:T(8,128)(2,1)S(1)}, s32[2,9]{1,0:T(2,128)S(4)}) custom-call(bf16[16,50304]{1,0:T(8,128)(2,1)} %volts_hbm.1, f32[392,384]{1,0:T(8,128)} %constant.2.clone.table_hbm, s32[16]{0:T(128)} %mask_hbm.1, s32[2,9]{1,0:T(2,128)} %bitcast.1), custom_call_target="tpu_custom_call" | custom-call | flops 905969664 | bytes 6291456 | tf_op jit(solution)/shard_map/exchange/pallas_call | solution.py:262
  32.0 3.2 %correlate.1 = bf16[9,3,2,256,256]{4,3,2,1,0:T(8,128)(2,1)} custom-call(s32[2,9]{1,0:T(2,128)S(4)} %get-tuple-element.7.table, bf16[128,3,16,256]{3,2,1,0:T(8,128)(2,1)S(1)} %get-tuple-element.8.spectra), custom_call_target="tpu_custom_call" | custom-call | flops 1811939328 | bytes 10485760 | tf_op jit(solution)/shard_map/correlate/pallas_call | solution.py:317

commit v6 on v5

--- a/solution.py
+++ b/solution.py
@@ -63,7 +63,7 @@
 
 CHUNKS = 4
 STEP = SPECTRA // CHUNKS
-PITCH = LOCAL + 8
+PITCH = LOCAL + 1
 
 
 def chunk(c):
@@ -72,18 +72,19 @@
 
 
 def channelize(volts_hbm, table_hbm, volts, table, dft, fir, spec, load, between):
-    loads = [pltpu.make_async_copy(table_hbm, table, load.at[CHUNKS])]
+    rows = 2 * BAND
+    loads = []
     for c in range(CHUNKS):
         loads.append(pltpu.make_async_copy(volts_hbm.at[:, chunk(c)], volts.at[:, chunk(c)], load.at[c]))
+    taps = pltpu.make_async_copy(table_hbm.at[pl.ds(2 * rows, 8)], table.at[pl.ds(2 * rows, 8)], load.at[CHUNKS + 3])
+    waves = pltpu.make_async_copy(table_hbm.at[pl.ds(0, 2 * rows)], table.at[pl.ds(0, 2 * rows)], load.at[CHUNKS])
+    taps.start()
+    loads[0].start()
     loads[1].start()
-    loads[0].start()
+    waves.start()
     for part in loads[2:]:
         part.start()
-    loads[0].wait()
-    rows = 2 * BAND
-    parts = table[0 : 2 * rows].astype(jnp.bfloat16)
-    dft[:, 0:PERIOD] = parts
-    dft[:, PERIOD:] = parts
+    taps.wait()
 
     def filt(step, carry):
         first = step * 8
@@ -96,13 +97,18 @@
             total = window[0] * frames[t]
             for m in range(1, TAPS):
                 total = total + window[m] * frames[t + m]
-            row = pl.multiple_of((first + t) * PITCH, 8)
+            row = (first + t) * PITCH
             for j in range(3):
                 fir[j, pl.ds(row, LOCAL), :] = total[:, j * 128 : (j + 1) * 128]
         return carry
 
     for c in range(CHUNKS):
-        loads[1 + c].wait()
+        loads[c].wait()
+        if c == CHUNKS - 1:
+            waves.wait()
+            parts = table[0 : 2 * rows].astype(jnp.bfloat16)
+            dft[:, 0:PERIOD] = parts
+            dft[:, PERIOD:] = parts
         lax.fori_loop(c * STEP // 8, (c + 1) * STEP // 8, filt, 0, unroll=True)
 
     between()
@@ -166,14 +172,14 @@
 
     def between():
         pl.when(z == 0)(greet_first)
-        pl.when(z == 3)(greet_others)
+        pl.when(z > 1)(greet_others)
 
     alive_load = pltpu.make_async_copy(mask_hbm, mask, load.at[CHUNKS + 1])
     alive_load.start()
     pairs_load = pltpu.make_async_copy(pairs_hbm, pairs, load.at[CHUNKS + 2])
     pairs_load.start()
     channelize(volts_hbm, table_hbm, volts, table, dft, fir, spec, load, between)
-    pl.when((z == 1) | (z == 2))(greet_others)
+    pl.when(z == 1)(greet_others)
     alive_load.wait()
     inputs = lax.broadcasted_iota(jnp.int32, (LOCAL, 1), 0)
     alive = jnp.zeros((LOCAL, 1), jnp.float32)
@@ -189,9 +195,9 @@
         pltpu.make_async_copy(blocks, blocks, sem).wait()
 
     def spread(ring, at, mine, others):
+        send(mine, out.at[at], s2, r2.at[ring], device(z, ahead(x, 2), y, c))
         send(others, out.at[at], s2, r2.at[ring], device(z, ahead(x, 1), y, c))
         send(others, out.at[at], s2, r2.at[ring], device(z, ahead(x, 3), y, c))
-        send(mine, out.at[at], s2, r2.at[ring], device(z, ahead(x, 2), y, c))
         send(mine, out.at[at], s3, r3, other_core)
 
     def prepare(dz):
@@ -236,7 +242,7 @@
         for dz in (3, 2, 1):
             depart(ahead(z, dz))
 
-    relay_on(z, NEAR)
+    relay_on(z, NEAR[:2])
 
     @pl.when(z == 0)
     def _():
@@ -244,9 +250,12 @@
         for zd in (3, 2, 1):
             depart(zd)
 
+    relay_on(z, NEAR[2:])
+    relay_on(order[0])
+    relay_on(order[1])
+    hand_over(z)
+    relay_on(order[2])
     for zs in order:
-        relay_on(zs)
-    for zs in [z] + order:
         hand_over(zs)
     arrived(out.at[pl.ds(0, 4 * RINGS)], r3)
     arrived(ready.at[pl.ds(0, RINGS - 1)], s1)
@@ -272,11 +281,11 @@
             pltpu.VMEM(table.shape, jnp.float32),
             pltpu.SMEM(mask.shape, jnp.int32),
             pltpu.VMEM((4 * BAND, 2 * PERIOD), jnp.bfloat16),
-            pltpu.VMEM((3, SPECTRA * PITCH, 128), jnp.float32),
-            pltpu.VMEM((2 * BAND * LOCAL, SPECTRA), jnp.float32),
+            pltpu.VMEM((3, (SPECTRA + 2) * PITCH // 8 * 8, 128), jnp.float32),
+            pltpu.VMEM(((2 * BAND + 1) * LOCAL, SPECTRA), jnp.float32),
             pltpu.VMEM((RINGS, 2, DEPTH, LOCAL, 2 * SPECTRA), jnp.bfloat16),
             pltpu.VMEM((RINGS, DEPTH, LOCAL, 2 * SPECTRA), jnp.bfloat16),
-            dma((CHUNKS + 3,)),
+            dma((CHUNKS + 4,)),
             dma,
             dma,
             dma,

time: 35.3 us -> 34.4 us (0.975)
  the two profiles are of different devices: /device:TPU:97 before, /device:TPU:1 now
where the time goes in v6:
time: 34.4 us; the launch traced here: 33.8 us
  Pallas kernels  33.8 us (98%)
    pallas_call x1, Pallas kernels, exchange(): pl.pallas_call(exchange_kernel, out_shape=(pltpu.VMEM((128, DEPTH, LOCAL,...  30.6 us
    pallas_call x1, Pallas kernels, correlate(): pl.pallas_call(correlate_kernel, out_shape=jax.ShapeDtypeStruct(shape, jn...  3.2 us

profile of v6, /device:TPU:1, one launch (start us, length us, event | category | flops | bytes accessed | tf_op | source)
XLA Modules:
  0.0 33.8 jit_solution(5067281019989180593)
XLA Ops:
  0.0 30.6 %exchange.1 = (bf16[128,3,16,256]{3,2,1,0:T(8,128)(2,1)S(1)}, s32[2,9]{1,0:T(2,128)S(4)}) custom-call(bf16[16,50304]{1,0:T(8,128)(2,1)} %volts_hbm.1, f32[392,384]{1,0:T(8,128)} %constant.2.clone.table_hbm, s32[16]{0:T(128)} %mask_hbm.1, s32[2,9]{1,0:T(2,128)} %bitcast.1), custom_call_target="tpu_custom_call" | custom-call | flops 905969664 | bytes 6291456 | tf_op jit(solution)/shard_map/exchange/pallas_call | solution.py:271
  30.6 3.2 %correlate.1 = bf16[9,3,2,256,256]{4,3,2,1,0:T(8,128)(2,1)} custom-call(s32[2,9]{1,0:T(2,128)S(4)} %get-tuple-element.7.table, bf16[128,3,16,256]{3,2,1,0:T(8,128)(2,1)S(1)} %get-tuple-element.8.spectra), custom_call_target="tpu_custom_call" | custom-call | flops 1811939328 | bytes 10485760 | tf_op jit(solution)/shard_map/correlate/pallas_call | solution.py:326

commit v7 on v6

--- a/solution.py
+++ b/solution.py
@@ -21,7 +21,7 @@
 GROUPS = BAND // DEPTH
 MESH = pl.DeviceIdType.MESH
 
-NEAR = (1, 3, 2)
+NEAR = (3, 1, 2)
 
 
 def tables():
@@ -71,7 +71,7 @@
     return pl.ds(first * PERIOD, ((c + 1) * STEP + TAPS - 1 - first) * PERIOD)
 
 
-def channelize(volts_hbm, table_hbm, volts, table, dft, fir, spec, load, between):
+def channelize(volts_hbm, table_hbm, volts, table, dft, fir, spec, load, enter, between):
     rows = 2 * BAND
     loads = []
     for c in range(CHUNKS):
@@ -84,6 +84,7 @@
     waves.start()
     for part in loads[2:]:
         part.start()
+    enter()
     taps.wait()
 
     def filt(step, carry):
@@ -153,13 +154,14 @@
         for dy in range(SIDE):
             signal(device(zd, x, ahead(y, dy), c))
 
-    for dy in NEAR:
-        signal(device(z, x, ahead(y, dy), c))
-    for d in (1, 2, 3):
-        signal(device(z, ahead(x, d), y, c))
-    signal(other_core)
-    for dz in (1, 2, 3):
-        pl.when((z > 0) & (ahead(z, dz) > 0))(lambda dz=dz: plane(ahead(z, dz)))
+    def enter():
+        for dy in NEAR:
+            signal(device(z, x, ahead(y, dy), c))
+        for d in (1, 2, 3):
+            signal(device(z, ahead(x, d), y, c))
+        signal(other_core)
+        for dz in (1, 2, 3):
+            pl.when((z > 0) & (ahead(z, dz) > 0))(lambda dz=dz: plane(ahead(z, dz)))
 
     def greet_first():
         pl.semaphore_wait(barrier, 7)
@@ -178,7 +180,7 @@
     alive_load.start()
     pairs_load = pltpu.make_async_copy(pairs_hbm, pairs, load.at[CHUNKS + 2])
     pairs_load.start()
-    channelize(volts_hbm, table_hbm, volts, table, dft, fir, spec, load, between)
+    channelize(volts_hbm, table_hbm, volts, table, dft, fir, spec, load, enter, between)
     pl.when(z == 1)(greet_others)
     alive_load.wait()
     inputs = lax.broadcasted_iota(jnp.int32, (LOCAL, 1), 0)

time: 34.4 us -> 34.1 us (level)
  Pallas kernels: 33.8 us -> 33.4 us
    pallas_call x1, Pallas kernels: 30.6 us -> 30.2 us  [exchange(): pl.pallas_call(exchange_kernel, out_shape=(pltpu.VMEM((128, DEPTH, LOCAL,...]
where the time goes in v7:
time: 34.1 us; the launch traced here: 33.4 us
  Pallas kernels  33.4 us (98%)
    pallas_call x1, Pallas kernels, exchange(): pl.pallas_call(exchange_kernel, out_shape=(pltpu.VMEM((128, DEPTH, LOCAL,...  30.2 us
    pallas_call x1, Pallas kernels, correlate(): pl.pallas_call(correlate_kernel, out_shape=jax.ShapeDtypeStruct(shape, jn...  3.2 us

profile of v7, /device:TPU:1, one launch (start us, length us, event | category | flops | bytes accessed | tf_op | source)
XLA Modules:
  0.0 33.4 jit_solution(4651307683426715770)
XLA Ops:
  0.0 30.2 %exchange.1 = (bf16[128,3,16,256]{3,2,1,0:T(8,128)(2,1)S(1)}, s32[2,9]{1,0:T(2,128)S(4)}) custom-call(bf16[16,50304]{1,0:T(8,128)(2,1)} %volts_hbm.1, f32[392,384]{1,0:T(8,128)} %constant.2.clone.table_hbm, s32[16]{0:T(128)} %mask_hbm.1, s32[2,9]{1,0:T(2,128)} %bitcast.1), custom_call_target="tpu_custom_call" | custom-call | flops 905969664 | bytes 6291456 | tf_op jit(solution)/shard_map/exchange/pallas_call | solution.py:273
  30.2 3.2 %correlate.1 = bf16[9,3,2,256,256]{4,3,2,1,0:T(8,128)(2,1)} custom-call(s32[2,9]{1,0:T(2,128)S(4)} %get-tuple-element.7.table, bf16[128,3,16,256]{3,2,1,0:T(8,128)(2,1)S(1)} %get-tuple-element.8.spectra), custom_call_target="tpu_custom_call" | custom-call | flops 1811939328 | bytes 10485760 | tf_op jit(solution)/shard_map/correlate/pallas_call | solution.py:328

commit v8 on v7

--- a/solution.py
+++ b/solution.py
@@ -174,14 +174,14 @@
 
     def between():
         pl.when(z == 0)(greet_first)
-        pl.when(z > 1)(greet_others)
+        pl.when((z > 1) & (y > 1))(greet_others)
 
     alive_load = pltpu.make_async_copy(mask_hbm, mask, load.at[CHUNKS + 1])
     alive_load.start()
     pairs_load = pltpu.make_async_copy(pairs_hbm, pairs, load.at[CHUNKS + 2])
     pairs_load.start()
     channelize(volts_hbm, table_hbm, volts, table, dft, fir, spec, load, enter, between)
-    pl.when(z == 1)(greet_others)
+    pl.when((z == 1) | ((z > 1) & (y < 2)))(greet_others)
     alive_load.wait()
     inputs = lax.broadcasted_iota(jnp.int32, (LOCAL, 1), 0)
     alive = jnp.zeros((LOCAL, 1), jnp.float32)

time: 34.1 us -> 34.2 us (level)
  the two profiles are of different devices: /device:TPU:1 before, /device:TPU:97 now
where the time goes in v8:
time: 34.2 us; the launch traced here: 34 us
  Pallas kernels  34 us (99%)
    pallas_call x1, Pallas kernels, exchange(): pl.pallas_call(exchange_kernel, out_shape=(pltpu.VMEM((128, DEPTH, LOCAL,...  30.8 us
    pallas_call x1, Pallas kernels, correlate(): pl.pallas_call(correlate_kernel, out_shape=jax.ShapeDtypeStruct(shape, jn...  3.19 us

profile of v8, /device:TPU:97, one launch (start us, length us, event | category | flops | bytes accessed | tf_op | source)
XLA Modules:
  0.0 34.0 jit_solution(7295317102079049533)
XLA Ops:
  0.0 30.8 %exchange.1 = (bf16[128,3,16,256]{3,2,1,0:T(8,128)(2,1)S(1)}, s32[2,9]{1,0:T(2,128)S(4)}) custom-call(bf16[16,50304]{1,0:T(8,128)(2,1)} %volts_hbm.1, f32[392,384]{1,0:T(8,128)} %constant.2.clone.table_hbm, s32[16]{0:T(128)} %mask_hbm.1, s32[2,9]{1,0:T(2,128)} %bitcast.1), custom_call_target="tpu_custom_call" | custom-call | flops 905969664 | bytes 6291456 | tf_op jit(solution)/shard_map/exchange/pallas_call | solution.py:273
  30.9 3.2 %correlate.1 = bf16[9,3,2,256,256]{4,3,2,1,0:T(8,128)(2,1)} custom-call(s32[2,9]{1,0:T(2,128)S(4)} %get-tuple-element.7.table, bf16[128,3,16,256]{3,2,1,0:T(8,128)(2,1)S(1)} %get-tuple-element.8.spectra), custom_call_target="tpu_custom_call" | custom-call | flops 1811939328 | bytes 10485760 | tf_op jit(solution)/shard_map/correlate/pallas_call | solution.py:328
